TPU v7x, 32 devices: a whole 2x2x4 slice. The times are simulated.
32 devices in a mesh: groups: 2 (over y), occ: 4 (over z), vir: 4 (over x, core).
Axes of the slice: x: 2, y: 2, z: 4, core: 2. Of those that a mesh axis runs over, the one named last changes fastest.
Arguments:
- amplitudes: bfloat16 [32, 400, 24, 128], P(('groups', 'occ'), None, 'vir'), parts along dimension 0, may hold values from -6 to 6
- amp_keep: int32 [32, 24], P(('groups', 'occ'), 'vir'), parts along dimension 0, may hold values 0 or 1
- integrals: bfloat16 [48, 128, 24, 128], P(('groups', 'vir')), parts along dimension 0, may hold values from -0.3125 to 0.3125
- int_keep: int32 [48, 24], P(('groups', 'vir')), parts along dimension 0, may hold values 0 or 1
- fock_vir: bfloat16 [48, 128, 128], P(('groups', 'vir')), parts along dimension 0, may hold values from -0.5 to 0.5
- fock_occ: bfloat16 [32, 400, 400], P(('groups', 'occ')), parts along dimension 0, may hold values from -0.3125 to 0.3125
- occ_energy: float32 [32, 400], P(('groups', 'occ')), parts along dimension 0, may hold values from -2 to -0.4
- vir_energy: float32 [48, 128], P(('groups', 'vir')), parts along dimension 0, may hold values from 0.4 to 3
- res_keep: int32 [32, 24], P(('groups', 'occ'), 'vir'), parts along dimension 0, may hold values 0 or 1
- res_place: int32 [32, 24], P(('groups', 'occ'), 'vir'), parts along dimension 0, may hold values from 0 to 95, as said below
Outputs:
- residual_tiles: float32 [192, 4, 400, 128], P(('groups', 'occ'), 'vir'), parts along dimension 0
- new_amplitudes: float32 [192, 4, 400, 128], P(('groups', 'occ'), 'vir'), parts along dimension 0
There are 2 independent parts, one for each index of `groups`. A program takes and returns all parts, laid end to end along the dimension named above; each array names one. Nothing has to cross between parts.
Inputs may be any that keep to these rules, and one draw needn't show every extreme that they name: Within each run of 6 virtual tiles, res_place maps the tiles of all pair tiles one to one onto 0 to 95. The tiles of one aligned run of 4 pair tiles within one such virtual run reach at most 6 values in any aligned run of 24 values, and exactly 6 in some.
All inputs are finite; a program needn't handle non-finite values. No bound on the sum of `amp_keep` or of `int_keep` or of `res_keep` on one device may be relied on, other than what follows from the above.
Results may differ from a plain program's by a relative error of at most 0.0003.
Values may be sent and summed in bfloat16 or wider, within the bound.
No kernel may reach another device: no remote copies, remote signals or barrier semaphores. Data moves between devices by JAX's collectives and lax.ppermute only.
A program may use at most 128 MiB of HBM per device.

v0:
```python
import collections
import functools

import jax
import jax.numpy as jnp
from jax import lax
from jax.experimental import pallas as pl
from jax.experimental.pallas import tpu as pltpu
from jax.sharding import PartitionSpec as P

CODE_ROWS = 16
LEVELS = 32700.0
MIB = 1024 * 1024
AMPS = 1024
FIELDS = 4
NOTE_ROWS = 16
PARTS = 3
HBM = pl.BlockSpec(memory_space=pltpu.HBM)
SMEM = pl.BlockSpec(memory_space=pltpu.SMEM)
VMEM = pl.BlockSpec(memory_space=pltpu.VMEM)
SIZE_NAMES = ("pairs", "rows", "blocks", "width", "dests", "runs", "tiles", "slots", "early", "extra")
SIZE_NAMES += ("starts", "entries")
Size = collections.namedtuple("Size", SIZE_NAMES)


def call(kernel, name, inputs, in_specs, out_shape, out_specs, scratch, vmem, aliases=None):
    return pl.pallas_call(
        kernel,
        out_shape=out_shape,
        in_specs=in_specs,
        out_specs=out_specs,
        scratch_shapes=scratch,
        input_output_aliases=aliases or {},
        compiler_params=pltpu.CompilerParams(vmem_limit_bytes=vmem * MIB),
        name=name,
    )(*inputs)


def chunk_of(size, slot):
    return sum((slot >= start).astype(jnp.int32) for start in size.starts[1:-1])


def scale_block(rows):
    return 80 if rows % 80 == 0 else rows


def encode(values, out):
    rows, width = values.shape
    block = scale_block(rows)
    cut = values.reshape(rows // block, block, width)
    top = jnp.max(jnp.abs(cut), axis=1, keepdims=True)
    step = jnp.clip(jnp.ceil(8.0 * jnp.log2(jnp.maximum(top, 1e-30))), -800.0, 800.0)
    whole = jnp.round(cut * (LEVELS * jnp.exp2(step * -0.125))).reshape(rows, width)
    out[:rows, :] = whole.astype(jnp.int32).astype(jnp.int16)
    steps = step.reshape(rows // block, width)
    steps = jnp.concatenate([steps, jnp.zeros((CODE_ROWS - rows // block, width), jnp.float32)], axis=0)
    out[rows:, :] = steps.astype(jnp.int32).astype(jnp.int16)


def decode(coded):
    rows, width = coded.shape[0] - CODE_ROWS, coded.shape[1]
    block = scale_block(rows)
    steps = coded[rows:, :].astype(jnp.int32).astype(jnp.float32)[: rows // block]
    scale = jnp.exp2(steps * 0.125) * (1.0 / LEVELS)
    whole = coded[:rows, :].astype(jnp.int32).astype(jnp.float32)
    return (whole.reshape(rows // block, block, width) * scale.reshape(rows // block, 1, width)).reshape(rows, width)


def plan_kernel(size, place_in, res_keep_in, amp_keep_in, int_keep_in, occ_energy, amps, *refs):
    late, spots, wanted, extra, mask_own, mask_send, packed = refs[:7]
    place, res_keep, amp_keep, int_keep, word_sem = refs[7:12]
    notes, early_at, res_count, amp_count, all_count, res_seen, stage, energies, note, come_sem, go_sem, note_sem = refs[12:]
    words_in = [
        pltpu.make_async_copy(source, target, word_sem.at[n])
        for n, (source, target) in enumerate(
            ((place_in, place), (res_keep_in, res_keep), (amp_keep_in, amp_keep), (int_keep_in, int_keep))
        )
    ]
    for copy in words_in:
        copy.start()
    me, core = lax.axis_index("occ"), lax.rem(lax.axis_index("vir"), 2)

    for s in range(size.dests):
        for ref in (res_count, amp_count, all_count, res_seen):
            ref[s] = 0
    for n in range(size.dests * size.extra):
        extra[n] = -1
    for n in range(size.dests * size.early):
        early_at[n] = -1

    def clear(n, carry):
        late[n] = -1
        spots[n] = 0
        for f in range(FIELDS):
            notes[n * FIELDS + f] = 0
        return carry

    lax.fori_loop(0, size.entries, clear, 0)
    for n in range(size.tiles):
        wanted[n] = -1
    for copy in words_in:
        copy.wait()

    res_seen[size.dests] = 0

    def entry(s, slot):
        at = s * size.starts[1] + slot
        for low, high in zip(size.starts[1:-1], size.starts[2:]):
            at = jnp.where(slot >= low, low * size.dests + s * (high - low) + slot - low, at)
        return at

    def aim(pair, column):
        where = place[pair, column]
        target = sum((where >= n * size.tiles).astype(jnp.int32) for n in range(1, size.dests))
        return target ^ me, where - target * size.tiles

    def residuals(pair, carry):
        for column in range(size.blocks):
            s, _ = aim(pair, column)

            @pl.when(res_keep[pair, column] != 0)
            def _(column=column, s=s):
                slot = res_count[s]
                res_count[s] = slot + 1
                late[entry(s, slot)] = pair * size.blocks + column

        return carry

    lax.fori_loop(0, size.pairs, residuals, 0)

    def amplitudes(pair, carry):
        for column in range(size.blocks):
            tile = pair * size.blocks + column
            s, owned = aim(pair, column)
            first = (s * size.slots + all_count[s]) * FIELDS
            all_count[s] = all_count[s] + 1
            notes[first] = owned + 1
            notes[first + 1] = tile
            notes[first + 2] = -1
            notes[first + 3] = -1

            @pl.when(res_keep[pair, column] != 0)
            def _(s=s, first=first):
                notes[first + 2] = res_seen[s]
                res_seen[s] = res_seen[s] + 1

            @pl.when(amp_keep[pair, column] != 0)
            def _(s=s, first=first, tile=tile):
                rank = amp_count[s]
                amp_count[s] = rank + 1
                slot = size.slots - 1 - (rank - size.early)

                @pl.when(rank < size.early)
                def _():
                    n = s * size.early + rank
                    early_at[n] = tile
                    notes[first + 3] = rank
                    pltpu.make_async_copy(amps.at[tile], stage.at[n], come_sem.at[n]).start()

                @pl.when((rank >= size.early) & (slot >= res_count[s]))
                def _():
                    late[entry(s, slot)] = tile + AMPS
                    notes[first + 3] = size.early + slot

                @pl.when((rank >= size.early) & (slot < res_count[s]))
                def _():
                    extra[s * size.extra + rank - size.early] = tile
                    notes[first + 3] = size.slots + rank
                    res_seen[size.dests] = 1

        return carry

    lax.fori_loop(0, size.pairs, amplitudes, 0)

    for s in range(size.dests):
        for slot in range(size.early):
            n = s * size.early + slot

            @pl.when(early_at[n] >= 0)
            def _(s=s, slot=slot, n=n):
                rows = pl.ds(slot * size.rows, size.rows)
                pltpu.make_async_copy(amps.at[0], stage.at[n], come_sem.at[n]).wait()
                pltpu.make_async_copy(stage.at[n], packed.at[me ^ s, rows], go_sem.at[n]).start()

    energies[...] = jnp.zeros((NOTE_ROWS, size.width), jnp.float32)
    strips = -(-size.rows // size.width)
    for pair in range(size.pairs):
        for strip in range(strips):
            low, high = strip * size.width, min(size.rows, (strip + 1) * size.width)
            energies[pair * strips + strip : pair * strips + strip + 1, : high - low] = occ_energy[pair : pair + 1, low:high]
    left = energies[...]
    lane = lax.broadcasted_iota(jnp.int32, (NOTE_ROWS, size.width), 1)
    parts = []
    for _ in range(PARTS):
        parts.append(left.astype(jnp.bfloat16))
        left = left - parts[-1].astype(jnp.float32)
    for s in range(size.dests):
        for n, part in enumerate(parts):
            note[s, n * NOTE_ROWS : (n + 1) * NOTE_ROWS] = part
        words = jnp.where(lane == size.slots * FIELDS, res_seen[size.dests], 0)
        for n in range(size.slots * FIELDS):
            words = jnp.where(lane == n, notes[s * size.slots * FIELDS + n], words)
        note[s, PARTS * NOTE_ROWS :] = words.astype(jnp.float32).astype(jnp.bfloat16)
        target = packed.at[me ^ s, pl.ds(size.early * size.rows, (PARTS + 1) * NOTE_ROWS)]
        pltpu.make_async_copy(note.at[s], target, note_sem.at[s]).start()

    def compact(n, count):
        what = late[n]
        kept = (what >= 0) & (what < AMPS)

        @pl.when(kept)
        def _():
            wanted[count] = what
            spots[n] = count

        return count + kept.astype(jnp.int32)

    lax.fori_loop(0, size.entries, compact, jnp.int32(0))

    for pair in range(size.pairs):
        mask = amp_keep[pair, 0]
        for block in range(1, size.blocks):
            mask = mask | (amp_keep[pair, block] << block)
        mask_own[pair] = mask
        mask_send[pair] = mask

    def integrals(run, carry):
        for column in range(size.blocks):
            for target, parity in ((mask_own, core), (mask_send, 1 - core)):
                at = (run * 2 + parity) * size.blocks + column
                mask = int_keep[0, at]
                for block in range(1, size.blocks):
                    mask = mask | (int_keep[block, at] << block)
                target[size.pairs + run * size.blocks + column] = mask
        return carry

    lax.fori_loop(0, size.runs, integrals, 0)

    for s in range(size.dests):
        for slot in range(size.early):
            n = s * size.early + slot

            @pl.when(early_at[n] >= 0)
            def _(s=s, slot=slot, n=n):
                pltpu.make_async_copy(stage.at[n], packed.at[0, pl.ds(0, size.rows)], go_sem.at[n]).wait()

        target = packed.at[0, pl.ds(0, (PARTS + 1) * NOTE_ROWS)]
        pltpu.make_async_copy(note.at[s], target, note_sem.at[s]).wait()


def integral_tile(ints, place, wide):
    for first in range(0, ints.shape[1], 8):

        @pl.when((place >= first) & (place < first + 8))
        def _(first=first):
            part = ints[:, first : first + 8, :].astype(jnp.float32)
            wide[...] = part.reshape(wide.shape)

    return wide[pl.ds(lax.rem(place, 8), ints.shape[0], stride=8), :].astype(ints.dtype)


def ladder(size, span, wanted, run, masks, sources, totals, work, more, last):
    active, amps, ints, wide, amp_sem, int_sem = work
    amp_copies, int_copies = [], []
    for part in range(2):
        amp_copies.append(pltpu.make_async_copy(sources[2 * part], amps.at[part], amp_sem.at[part]))
        amp_copies[-1].start()
        int_copies.append([])
        for block in range(size.blocks):
            source = sources[2 * part + 1].at[block]
            int_copies[-1].append(pltpu.make_async_copy(source, ints.at[part, block], int_sem.at[part, block]))
            int_copies[-1][-1].start()
    core = lax.rem(lax.axis_index("vir"), 2)

    def prepare(n, carry):
        tile = wanted[n]
        active[n] = 0

        @pl.when(tile >= 0)
        def _():
            pair, column = tile // size.blocks, lax.rem(tile, size.blocks)
            at = size.pairs + run * size.blocks + column
            both = (masks[0][pair] & masks[0][at]) | ((masks[1][pair] & masks[1][at]) << size.blocks)
            active[n] = both
            totals[n] = jnp.zeros((size.rows, size.width), jnp.float32)

        return carry

    lax.fori_loop(*span, prepare, 0)
    for part in range(2):
        amp_copies[part].wait()
        if part == 0 and more is not None:

            def add_more(n, carry):
                @pl.when(wanted[n] >= 0)
                def _():
                    more(wanted[n], totals.at[n], amps.at[0])

                return carry

            lax.fori_loop(*span, add_more, 0)
        for block in range(size.blocks):
            int_copies[part][block].wait()
            bit = 1 << (part * size.blocks + block)

            def add(n, carry, part=part, block=block, bit=bit):
                @pl.when((active[n] & bit) != 0)
                def _():
                    tile = wanted[n]
                    pair, column = tile // size.blocks, lax.rem(tile, size.blocks)
                    place = (run * 2 + core) * size.blocks + column
                    totals[n] += jnp.dot(
                        amps[part, pair * size.blocks + block],
                        integral_tile(ints.at[part, block], place, wide),
                        preferred_element_type=jnp.float32,
                    )

                return carry

            lax.fori_loop(*span, add, 0)

    def leave(n, carry):
        @pl.when(wanted[n] >= 0)
        def _():
            last(n, totals.at[n])

        return carry

    lax.fori_loop(*span, leave, 0)


def sums_kernel(size, pieces, step, wanted, mask_own, mask_other, amps_own, ints_own, amps_other, ints_other, *refs):
    outs, refs = refs[: len(pieces)], refs[len(pieces) :]
    totals, work, (stage, sem) = refs[0], refs[1:7], refs[7:]
    run = (lax.axis_index("vir") // 2) ^ step
    span = (pieces[0][0], pieces[-1][1])

    def send(n, total):
        encode(total[...], stage.at[n])
        for out, (low, high) in zip(outs, pieces):

            @pl.when((n >= low) & (n < high))
            def _(out=out, low=low):
                pltpu.make_async_copy(stage.at[n], out.at[n - low], sem.at[n]).start()

    sources = (amps_own, ints_own, amps_other, ints_other)
    ladder(size, span, wanted, run, (mask_own, mask_other), sources, totals, work, None, send)

    def finish(n, carry):
        @pl.when(wanted[n] >= 0)
        def _():
            pltpu.make_async_copy(stage.at[n], outs[0].at[0], sem.at[n]).wait()

        return carry

    lax.fori_loop(*span, finish, 0)


def own_kernel(
    size, span, wanted, mask_own, mask_other, amps_own, ints_own, amps_other, ints_other, fock_vir, fock_occ, out, *refs
):
    totals, work, sem = refs[0], refs[1:7], refs[7]
    run = lax.axis_index("vir") // 2

    def fock(tile, total, amps):
        pair, column = tile // size.blocks, lax.rem(tile, size.blocks)

        @pl.when(((mask_own[pair] >> column) & 1) != 0)
        def _():
            kept = amps[tile]
            total[...] += jnp.dot(kept, fock_vir[column], preferred_element_type=jnp.float32)
            total[...] -= jnp.dot(fock_occ[pair], kept, preferred_element_type=jnp.float32)

    def send(n, total):
        pltpu.make_async_copy(total, out.at[n - span[0]], sem.at[n]).start()

    sources = (amps_own, ints_own, amps_other, ints_other)
    ladder(size, span, wanted, run, (mask_own, mask_other), sources, totals, work, fock, send)

    def finish(n, carry):
        @pl.when(wanted[n] >= 0)
        def _():
            pltpu.make_async_copy(totals.at[n], out.at[0], sem.at[n]).wait()

        return carry

    lax.fori_loop(*span, finish, 0)


def join_kernel(size, chunk, pieces, own_spans, others, late, spots, amps, *refs):
    own, refs = refs[: len(own_spans)], refs[len(own_spans) :]
    came, refs = refs[: others * len(pieces)], refs[others * len(pieces) :]
    outs, refs = refs[:-8], refs[-8:]
    own_here, came_here, amps_here, stage, own_sem, came_sem, amps_sem, out_sem = refs
    per_dest = size.starts[chunk + 1] - size.starts[chunk]
    first, many = size.starts[chunk] * size.dests, per_dest * size.dests

    def fetch(n, carry):
        what, spot = late[first + n], spots[first + n]

        @pl.when((what >= 0) & (what < AMPS))
        def _():
            for part, (low, high) in zip(own, own_spans):

                @pl.when((spot >= low) & (spot < high))
                def _(part=part, low=low):
                    pltpu.make_async_copy(part.at[spot - low], own_here.at[n], own_sem.at[n]).start()

            for k in range(others):
                for piece, (low, high) in enumerate(pieces):

                    @pl.when((spot >= low) & (spot < high))
                    def _(k=k, piece=piece, low=low):
                        source = came[k * len(pieces) + piece]
                        pltpu.make_async_copy(source.at[spot - low], came_here.at[k, n], came_sem.at[k, n]).start()

        @pl.when(what >= AMPS)
        def _():
            pltpu.make_async_copy(amps.at[what - AMPS], amps_here.at[n], amps_sem.at[n]).start()

        return carry

    def send(n):
        if len(outs) == 1:
            target = outs[0].at[(n // per_dest) ^ lax.axis_index("occ"), lax.rem(n, per_dest)]
            pltpu.make_async_copy(stage.at[n], target, out_sem.at[n]).start()
            return
        for s in range(size.dests):

            @pl.when(n // per_dest == s)
            def _(s=s):
                slot = lax.rem(n, per_dest)
                pltpu.make_async_copy(stage.at[n], outs[s].at[slot], out_sem.at[n]).start()

    def make(n, carry):
        what = late[first + n]

        @pl.when((what >= 0) & (what < AMPS))
        def _():
            pltpu.make_async_copy(own[0].at[0], own_here.at[n], own_sem.at[n]).wait()
            total = own_here[n]
            for k in range(others):
                pltpu.make_async_copy(came[0].at[0], came_here.at[k, n], came_sem.at[k, n]).wait()
                total = total + decode(came_here[k, n])
            encode(total, stage.at[n])
            send(n)

        @pl.when(what >= AMPS)
        def _():
            pltpu.make_async_copy(amps.at[0], amps_here.at[n], amps_sem.at[n]).wait()
            encode(amps_here[n].astype(jnp.float32), stage.at[n])
            send(n)

        return carry

    def finish(n, carry):
        @pl.when(late[first + n] >= 0)
        def _():
            target = outs[0].at[0, 0] if len(outs) == 1 else outs[0].at[0]
            pltpu.make_async_copy(stage.at[n], target, out_sem.at[n]).wait()

        return carry

    lax.fori_loop(0, many, fetch, 0)
    lax.fori_loop(0, many, make, 0)
    lax.fori_loop(0, many, finish, 0)


def pack_kernel(size, table, amps, *refs):
    outs, (stage, come_sem, go_sem) = refs[: size.dests], refs[size.dests :]

    def each(act):
        for s in range(size.dests):
            for slot in range(size.extra):
                n = s * size.extra + slot

                @pl.when(table[n] >= 0)
                def _(s=s, slot=slot, n=n):
                    act(s, slot, n)

    def come(s, slot, n):
        return pltpu.make_async_copy(amps.at[jnp.maximum(table[n], 0)], stage.at[n], come_sem.at[n])

    def go(s, slot, n):
        return pltpu.make_async_copy(stage.at[n], outs[s].at[slot], go_sem.at[n])

    def turn(*at):
        come(*at).wait()
        go(*at).start()

    each(lambda *at: come(*at).start())
    each(turn)
    each(lambda *at: go(*at).wait())


def final_kernel(size, counts, with_extra, first, last, buffers, notes, occ_cols, vir_energy, amps, *refs):
    codes = []
    for count in counts:
        codes.append(refs[:count])
        refs = refs[count:]
    me = lax.axis_index("occ")
    one_code = codes[0][0].at[0] if counts[0] > 1 else codes[0][0].at[0, 0]
    one_amps = amps.at[0, pl.ds(0, size.rows)]
    more = refs[: size.dests] if with_extra else None
    out_res, out_upd, slot_of, col_of, row_of, kind_of, has_res, res_here, code_here, amps_here, made = refs[-14:-3]
    res_sem, amps_sem, go_sem = refs[-3:]
    rows, width = made.shape[2], made.shape[3]

    def fetch_code(s, slot, target, sem):
        for chunk, parts in enumerate(codes):

            @pl.when(chunk_of(size, slot) == chunk)
            def _(chunk=chunk, parts=parts):
                at = slot - size.starts[chunk]
                source = parts[s].at[at] if len(parts) > 1 else parts[0].at[s ^ me, at]
                pltpu.make_async_copy(source, target, sem).start()

    for s in range(size.dests):

        def fetch(n, carry, s=s):
            at = s * size.slots + n
            source = s ^ me
            owned, tile, res_slot, amp_slot = (notes[source, n * FIELDS + f] for f in range(FIELDS))
            amp_late = amp_slot - size.early
            is_late = (amp_late >= 0) & (amp_late < size.slots)
            is_extra = amp_late >= size.slots
            is_early = (amp_slot >= 0) & (amp_slot < size.early)
            needs = jnp.maximum(
                jnp.where(res_slot >= 0, chunk_of(size, res_slot), 0),
                jnp.where(is_extra, len(size.starts) - 2, jnp.where(is_late, chunk_of(size, amp_late), 0)),
            )
            mine = (owned > 0) & (needs >= first) & (needs <= last)
            slot_of[at] = jnp.where(mine, owned - 1, -1)
            pair = tile // size.blocks
            col_of[at] = source * size.pairs + pair
            row_of[at] = tile - pair * size.blocks
            kind_of[at] = jnp.where(is_late, 2, jnp.where(amp_slot >= 0, 1, 0))
            has_res[at] = (res_slot >= 0).astype(jnp.int32)

            @pl.when(mine & (res_slot >= 0))
            def _():
                fetch_code(s, res_slot, res_here.at[at], res_sem.at[at])

            @pl.when(mine & is_early)
            def _():
                place = pl.ds(pl.multiple_of(amp_slot * size.rows, 16), size.rows)
                pltpu.make_async_copy(amps.at[source, place], amps_here.at[at], amps_sem.at[at]).start()

            @pl.when(mine & is_late)
            def _():
                fetch_code(s, amp_late, code_here.at[at], amps_sem.at[at])

            if with_extra:

                @pl.when(mine & is_extra)
                def _():
                    spare = more[s].at[amp_late - size.slots]
                    pltpu.make_async_copy(spare, amps_here.at[at], amps_sem.at[at]).start()

            return carry

        lax.fori_loop(0, size.slots, fetch, 0)

    def leave(slot, buffer):
        return (
            pltpu.make_async_copy(made.at[buffer, 0], out_res.at[slot, 0], go_sem.at[buffer, 0]),
            pltpu.make_async_copy(made.at[buffer, 1], out_upd.at[slot, 0], go_sem.at[buffer, 1]),
        )

    def step(at, count):
        slot = slot_of[at]
        mine = slot >= 0
        buffer = lax.rem(count, buffers)

        @pl.when(mine)
        def _():
            @pl.when(count >= buffers)
            def _():
                for copy in leave(0, buffer):
                    copy.wait()

            kind = kind_of[at]

            @pl.when(kind == 0)
            def _():
                made[buffer, 1] = jnp.zeros((rows, width), jnp.float32)

            @pl.when(kind == 1)
            def _():
                pltpu.make_async_copy(one_amps, amps_here.at[at], amps_sem.at[at]).wait()
                made[buffer, 1] = amps_here[at].astype(jnp.float32)

            @pl.when(kind == 2)
            def _():
                pltpu.make_async_copy(one_code, code_here.at[at], amps_sem.at[at]).wait()
                made[buffer, 1] = decode(code_here[at])

            @pl.when(has_res[at] == 0)
            def _():
                made[buffer, 0] = jnp.zeros((rows, width), jnp.float32)

            @pl.when(has_res[at] != 0)
            def _():
                pltpu.make_async_copy(one_code, res_here.at[at], res_sem.at[at]).wait()
                resid = decode(res_here[at])
                lane = lax.broadcasted_iota(jnp.int32, (rows, width), 1)
                occ = jnp.sum(jnp.where(lane == col_of[at], occ_cols[...], 0.0), axis=1, keepdims=True)
                vir = vir_energy[pl.ds(row_of[at], 1), :]
                made[buffer, 0] = resid
                made[buffer, 1] += resid / (vir - occ)

            for copy in leave(slot, buffer):
                copy.start()

        return count + mine.astype(jnp.int32)

    count = lax.fori_loop(0, size.dests * size.slots, step, jnp.int32(0))
    for buffer in range(buffers):

        @pl.when(buffer < count)
        def _(buffer=buffer):
            for copy in leave(0, buffer):
                copy.wait()


def body(
    amplitudes,
    amp_keep,
    integrals,
    int_keep,
    fock_vir,
    fock_occ,
    occ_energy,
    vir_energy,
    res_keep,
    res_place,
):
    pairs, rows, blocks, width = amplitudes.shape
    dests, virs = lax.axis_size("occ"), lax.axis_size("vir")
    runs = virs // 2
    tiles = pairs * blocks
    slots = max(2, (tiles + dests - 1) // dests)
    early = max(1, 2 * slots // 3)
    starts = (0, slots // 3, slots * 2 // 3, slots) if slots % 3 == 0 else (0, 1, slots)
    chunks = len(starts) - 1
    entries = slots * dests
    size = Size(
        pairs, rows, blocks, width, dests, runs, tiles, slots, early, slots - early, starts, entries
    )
    coded = (rows + CODE_ROWS, width)
    plain = (rows, width)

    def swap(array, axis, bit):
        return lax.ppermute(array, axis, [(i, i ^ bit) for i in range(lax.axis_size(axis))])

    def words(count):
        return jax.ShapeDtypeStruct((count,), jnp.int32)

    def counters(count):
        return pltpu.SMEM((count,), jnp.int32)

    dma = pltpu.SemaphoreType.DMA

    amps = jnp.transpose(amplitudes, (0, 2, 1, 3)).reshape(tiles, rows, width)
    amps_other = swap(amps, "vir", 1)
    ints_other = swap(integrals, "vir", 1)

    sent_rows = early * rows + (PARTS + 1) * NOTE_ROWS
    late, spots, wanted, extra, mask_own, mask_send, packed = call(
        functools.partial(plan_kernel, size),
        "plan_tiles",
        (res_place, res_keep, amp_keep, int_keep, occ_energy, amps),
        [HBM] * 4 + [VMEM, HBM],
        [
            words(size.entries),
            words(size.entries),
            words(tiles),
            words(dests * size.extra),
            words(pairs + runs * blocks),
            words(pairs + runs * blocks),
            jax.ShapeDtypeStruct((dests, sent_rows, width), amps.dtype),
        ],
        [SMEM] * 6 + [HBM],
        [pltpu.SMEM(a.shape, jnp.int32) for a in (res_place, res_keep, amp_keep, int_keep)]
        + [dma((4,)), counters(dests * slots * FIELDS), counters(dests * early)]
        + [counters(dests)] * 3
        + [
            counters(dests + 1),
            pltpu.VMEM((dests * early, *plain), amps.dtype),
            pltpu.VMEM((NOTE_ROWS, width), jnp.float32),
            pltpu.VMEM((dests, (PARTS + 1) * NOTE_ROWS, width), amps.dtype),
            dma((dests * early,)),
            dma((dests * early,)),
            dma((dests,)),
        ],
        55,
    )
    wanted_other = [swap(wanted, "vir", 2 * k) for k in range(1, runs)]
    amps_came = lax.all_to_all(packed, "occ", split_axis=0, concat_axis=0, tiled=True)
    mask_other = swap(mask_send, "vir", 1)

    shared = (mask_own, mask_other, amps, integrals, amps_other, ints_other)
    share_specs = [SMEM] * 2 + [HBM] * 4
    work = [
        pltpu.VMEM((tiles, *plain), jnp.float32),
        counters(tiles),
        pltpu.VMEM((2, *amps.shape), amps.dtype),
        pltpu.VMEM((2, *integrals.shape), integrals.dtype),
        pltpu.VMEM((8 * width, width), jnp.float32),
        dma((2,)),
        dma((2, blocks)),
    ]

    bounds = [min(tiles, start * dests) for start in starts[1:-1]]
    bounds = sorted({0, *bounds, max(bounds[-1], tiles - tiles // 6), tiles})
    pieces = list(zip(bounds[:-1], bounds[1:]))
    rare = pieces[-1][0] >= tiles - tiles // 6 and len(pieces) > 1
    sums_came = []
    for k in range(1, runs):
        sums = []
        for some in (pieces[:1], pieces[1:]):
            if some:
                sums += call(
                    functools.partial(sums_kernel, size, some, k),
                    "ladder_sums",
                    (wanted_other[k - 1], *shared),
                    [SMEM] + share_specs,
                    [jax.ShapeDtypeStruct((high - low, *coded), jnp.int16) for low, high in some],
                    [HBM] * len(some),
                    [*work, pltpu.VMEM((tiles, *coded), jnp.int16), dma((tiles,))],
                    55,
                )
        came = [swap(part, "vir", 2 * k) for part in (sums[:-1] if rare else sums)]
        if rare:
            came.append(sums[-1])
        sums_came.append(came)

    def own_part(span, wanted):
        return call(
            functools.partial(own_kernel, size, span),
            "own_part",
            (wanted, *shared, fock_vir, fock_occ),
            [SMEM] + share_specs + [VMEM] * 2,
            jax.ShapeDtypeStruct((span[1] - span[0], *plain), jnp.float32),
            HBM,
            [*work, dma((tiles,))],
            55,
        )

    buffers = 4
    own_spans = [pieces[0]] + ([(pieces[0][1], tiles)] if len(pieces) > 1 else [])
    own = [own_part(own_spans[0], wanted)]

    codes = []
    for c in range(chunks):
        use = pieces if c == chunks - 1 else pieces[: min(c + 1, len(pieces))]
        per_dest = starts[c + 1] - starts[c]
        per_chunk = per_dest * dests
        if rare and c == chunks - 1:
            for k in range(1, runs):
                part, mine, theirs, _ = lax.optimization_barrier((sums_came[k - 1][-1], wanted, wanted_other[k - 1], joined[0]))
                beyond = (mine[use[-1][0]] >= 0) | (theirs[use[-1][0]] >= 0)
                sums_came[k - 1][-1] = lax.cond(
                    beyond, functools.partial(swap, axis="vir", bit=2 * k), lambda part: part, part
                )
        came = [part for parts in sums_came for part in parts[: len(use)]]
        if codes:
            late, after, _ = lax.optimization_barrier((late, wanted, joined[0]))
            if len(own) < len(own_spans):
                own.append(own_part(own_spans[1], after))
        spread = True
        outs = dests if spread else 1
        joined = call(
            functools.partial(join_kernel, size, c, use, own_spans[: len(own)], runs - 1),
            "join_parts",
            (late, spots, amps, *own, *came),
            [SMEM] * 2 + [HBM] * (1 + len(own) + len(came)),
            [jax.ShapeDtypeStruct((per_dest, *coded) if spread else (dests, per_dest, *coded), jnp.int16)] * outs,
            [HBM] * outs,
            [
                pltpu.VMEM((per_chunk, *plain), jnp.float32),
                pltpu.VMEM((runs - 1, per_chunk, *coded), jnp.int16),
                pltpu.VMEM((per_chunk, *plain), amps.dtype),
                pltpu.VMEM((per_chunk, *coded), jnp.int16),
                dma((per_chunk,)),
                dma((runs - 1, per_chunk)),
                dma((per_chunk,)),
                dma((per_chunk,)),
            ],
            60,
        )
        if spread:
            codes.append([joined[0]] + [swap(joined[s], "occ", s) for s in range(1, dests)])
        else:
            codes.append([lax.all_to_all(joined[0], "occ", split_axis=0, concat_axis=0, tiled=True)])

    amps_came, _ = lax.optimization_barrier((amps_came, codes[0][0]))
    said = amps_came[:, early * rows :].reshape(dests, PARTS + 1, NOTE_ROWS, width).astype(jnp.float32)
    strips = -(-rows // width)
    occ_all = (said[:, 0] + said[:, 1] + said[:, 2])[:, : pairs * strips].reshape(dests * pairs, strips * width)[:, :rows]
    occ_cols = jnp.transpose(jnp.pad(occ_all, ((0, width - dests * pairs), (0, 0))))
    notes = said[:, PARTS, 0].astype(jnp.int32)
    over = jnp.max(notes[:, slots * FIELDS]) > 0

    def finish(first, last, more, results):
        have = [code for part in codes[: last + 1] for code in part]
        inputs = (notes, occ_cols, vir_energy, amps_came, *have, *more, *results)
        counts = tuple(len(part) for part in codes[: last + 1])
        many = dests * slots
        return call(
            functools.partial(final_kernel, size, counts, bool(more), first, last, buffers),
            "update_tiles",
            inputs,
            [SMEM] + [VMEM] * 2 + [HBM] * (len(inputs) - 3),
            [jax.ShapeDtypeStruct((tiles, 1, *plain), jnp.float32)] * 2,
            [HBM] * 2,
            [counters(many)] * 5
            + [
                pltpu.VMEM((many, *coded), jnp.int16),
                pltpu.VMEM((many, *coded), jnp.int16),
                pltpu.VMEM((many, *plain), amps.dtype),
                pltpu.VMEM((buffers, 2, *plain), jnp.float32),
                dma((many,)),
                dma((many,)),
                dma((buffers, 2)),
            ],
            60,
            {len(inputs) - 2: 0, len(inputs) - 1: 1} if results else None,
        )

    results = finish(0, 0, [], ())

    def with_extra(results):
        more = call(
            functools.partial(pack_kernel, size),
            "pack_extra",
            (extra, amps),
            [SMEM, HBM],
            [jax.ShapeDtypeStruct((size.extra, *plain), amps.dtype)] * dests,
            [HBM] * dests,
            [
                pltpu.VMEM((dests * size.extra, *plain), amps.dtype),
                dma((dests * size.extra,)),
                dma((dests * size.extra,)),
            ],
            60,
        )
        more = [more[0]] + [swap(more[s], "occ", s) for s in range(1, dests)]
        return tuple(finish(1, chunks - 1, more, results))

    def without_extra(results):
        return tuple(finish(1, chunks - 1, [], results))

    return lax.cond(over, with_extra, without_extra, tuple(results))


def solution(mesh):
    return jax.shard_map(
        body,
        mesh=mesh,
        in_specs=(
            P(("groups", "occ"), None, "vir", None),
            P(("groups", "occ"), "vir"),
            P(("groups", "vir"), None, None, None),
            P(("groups", "vir"), None),
            P(("groups", "vir"), None, None),
            P(("groups", "occ"), None, None),
            P(("groups", "occ"), None),
            P(("groups", "vir"), None),
            P(("groups", "occ"), "vir"),
            P(("groups", "occ"), "vir"),
        ),
        out_specs=(
            P(("groups", "occ"), "vir", None, None),
            P(("groups", "occ"), "vir", None, None),
        ),
        check_vma=False,
    )
```

profile of v0, /device:TPU:8, one launch (start us, length us, event | category | flops | bytes accessed | tf_op | source)
XLA Modules:
  0.0 121.3 jit_solution(6222672898808675294)
XLA Ops:
  1.2 5.3 %plan_tiles.1 = (s32[24]{0:T(128)}, s32[24]{0:T(128)}, s32[24]{0:T(128)}, s32[8]{0:T(128)S(1)}, s32[16]{0:T(128)}, /*index=5*/s32[16]{0:T(128)}, bf16[4,1664,128]{2,1,0:T(8,128)(2,1)}) custom-call(s32[4,6]{1,0:T(4,128)} %place_in.1, s32[4,6]{1,0:T(4,128)} %res_keep_in.1, s32[4,6]{1,0:T(4,128)} %amp_keep_in.1, s32[6,24]{1,0:T(8,128)} %int_keep_in.1, ...), custom_call_target="tpu_custom_call" | custom-call | tf_op jit(solution)/shard_map/plan_tiles/pallas_call | solution.py:27
  6.5 5.5 %all-to-all-start = ((bf16[4,1664,128]{2,1,0:T(8,128)(2,1)}), bf16[4,1664,128]{2,1,0:T(8,128)(2,1)}, u32[]{:S(2)}, u32[]{:S(2)}) async-start(bf16[4,1664,128]{2,1,0:T(8,128)(2,1)} %get-tuple-element.156), calls=%async_computation | async-start | bytes 3407872 | tf_op jit(solution)/shard_map/all_to_all | solution.py:699
  12.0 1.2 %collective-permute-start.7 = (s32[24]{0:T(128)}, s32[24]{0:T(128)S(1)}, u32[]{:S(2)}, u32[]{:S(2)}) collective-permute-start(s32[24]{0:T(128)} %get-tuple-element.177.wanted), channel_id=1, source_target_pairs={{0,2},{1,3},{2,0},{3,1},{4,6},{5,7},{6,4},{7,5},{8,10},{9,11},{10,... | collective-permute-start | bytes 296 | tf_op jit(solution)/shard_map/ppermute | solution.py:654
  13.3 2.5 %collective-permute-done.7.wanted = s32[24]{0:T(128)S(1)} collective-permute-done((s32[24]{0:T(128)}, s32[24]{0:T(128)S(1)}, u32[]{:S(2)}, u32[]{:S(2)}) %collective-permute-start.7) | collective-permute-done | bytes 128 | tf_op jit(solution)/shard_map/ppermute | solution.py:654
  16.3 6.9 %ladder_sums.2 = s16[8,416,128]{2,1,0:T(8,128)(2,1)} custom-call(s32[24]{0:T(128)} %copy-done.7, s32[16]{0:T(128)} %get-tuple-element.160.mask_own, s32[16]{0:T(128)} %copy-done.6, bf16[24,400,128]{2,1,0:T(8,128)(2,1)S(1)} %bitcast.32, bf16[6,128,24,128]{3,2,1,0:T(8,128)(2,1)} %ints_own.7, bf16[24,400,128]{2,1,0:T(8,128)(2,1)} %collective-permute-done.5.amps_other, ...), custom_call_target="tpu_custom_call" | custom-call | tf_op jit(solution)/shard_map/ladder_sums/pallas_call | solution.py:27
  23.2 3.2 %collective-permute-start.8 = (s16[8,416,128]{2,1,0:T(8,128)(2,1)}, s16[8,416,128]{2,1,0:T(8,128)(2,1)S(1)}, u32[]{:S(2)}, u32[]{:S(2)}) collective-permute-start(s16[8,416,128]{2,1,0:T(8,128)(2,1)} %ladder_sums.2), channel_id=1, source_target_pairs={{0,2},{1,3},{2,0},{3,1},{4,6},{5,7},{6,4},{7,5},{8,10},{9,11},{10,... | collective-permute-start | bytes 2555912 | tf_op jit(solution)/shard_map/ppermute | solution.py:654
  26.4 6.4 %ladder_sums.3 = (s16[8,416,128]{2,1,0:T(8,128)(2,1)}, s16[4,416,128]{2,1,0:T(8,128)(2,1)}, s16[4,416,128]{2,1,0:T(8,128)(2,1)}) custom-call(s32[24]{0:T(128)} %copy-done.7, s32[16]{0:T(128)} %get-tuple-element.160.mask_own, s32[16]{0:T(128)} %copy-done.6, bf16[24,400,128]{2,1,0:T(8,128)(2,1)S(1)} %bitcast.33, bf16[6,128,24,128]{3,2,1,0:T(8,128)(2,1)} %ints_own.7, ...), custom_call_target="tpu_custom_call" | custom-call | tf_op jit(solution)/shard_map/ladder_sums/pallas_call | solution.py:27
  32.9 1.6 %collective-permute-start.12 = (s16[8,416,128]{2,1,0:T(8,128)(2,1)}, s16[8,416,128]{2,1,0:T(8,128)(2,1)}, u32[]{:S(2)}, u32[]{:S(2)}) collective-permute-start(s16[8,416,128]{2,1,0:T(8,128)(2,1)} %get-tuple-element.169), channel_id=1, source_target_pairs={{0,2},{1,3},{2,0},{3,1},{4,6},{5,7},{6,4},{7,5},{8,10},{9,11},{10,... | collective-permute-start | bytes 2555912 | tf_op jit(solution)/shard_map/ppermute | solution.py:654
  34.9 9.0 %own_part.2.refs_0_ = f32[8,400,128]{2,1,0:T(8,128)} custom-call(s32[24]{0:T(128)} %get-tuple-element.177.wanted, s32[16]{0:T(128)} %get-tuple-element.160.mask_own, s32[16]{0:T(128)} %copy-done.6, bf16[24,400,128]{2,1,0:T(8,128)(2,1)S(1)} %bitcast.34, bf16[6,128,24,128]{3,2,1,0:T(8,128)(2,1)} %ints_own.7, ...), custom_call_target="tpu_custom_call" | custom-call | tf_op jit(solution)/shard_map/own_part/pallas_call | solution.py:27
  43.9 2.5 %collective-permute-done.8.refs_1_.refs_2_ = s16[8,416,128]{2,1,0:T(8,128)(2,1)S(1)} collective-permute-done((s16[8,416,128]{2,1,0:T(8,128)(2,1)}, s16[8,416,128]{2,1,0:T(8,128)(2,1)S(1)}, u32[]{:S(2)}, u32[]{:S(2)}) %collective-permute-start.8) | collective-permute-done | bytes 852000 | tf_op jit(solution)/shard_map/ppermute | solution.py:654
  46.4 0.9 copy-done.1
  47.3 3.6 %join_parts.3 = (s16[2,416,128]{2,1,0:T(8,128)(2,1)S(1)}, s16[2,416,128]{2,1,0:T(8,128)(2,1)}, s16[2,416,128]{2,1,0:T(8,128)(2,1)}, s16[2,416,128]{2,1,0:T(8,128)(2,1)}) custom-call(s32[24]{0:T(128)} %get-tuple-element.174.late, s32[24]{0:T(128)} %get-tuple-element.158.spots, bf16[24,400,128]{2,1,0:T(8,128)(2,1)S(1)} %bitcast.35, ...), custom_call_target="tpu_custom_call" | custom-call | tf_op jit(solution)/shard_map/join_parts/pallas_call | solution.py:27
  50.9 0.9 slice.27
  51.8 1.2 collective-permute-start.9
  53.0 2.8 %collective-permute-start.10 = (s16[2,416,128]{2,1,0:T(8,128)(2,1)}, s16[2,416,128]{2,1,0:T(8,128)(2,1)S(1)}, u32[]{:S(2)}, u32[]{:S(2)}) collective-permute-start(s16[2,416,128]{2,1,0:T(8,128)(2,1)} %get-tuple-element.165), channel_id=1, source_target_pairs={{0,8},{4,12},{8,0},{12,4},{1,9},{5,13},{9,1},{13,5},{2,10},{6,14},... | collective-permute-start | bytes 638984 | tf_op jit(solution)/shard_map/ppermute | solution.py:654
  55.8 7.3 %own_part.3.refs_1_ = f32[16,400,128]{2,1,0:T(8,128)} custom-call(s32[24]{0:T(128)} %get-tuple-element.177.wanted, s32[16]{0:T(128)} %get-tuple-element.160.mask_own, s32[16]{0:T(128)} %copy-done.6, bf16[24,400,128]{2,1,0:T(8,128)(2,1)S(1)} %bitcast.36, bf16[6,128,24,128]{3,2,1,0:T(8,128)(2,1)} %ints_own.7, ...), custom_call_target="tpu_custom_call" | custom-call | tf_op jit(solution)/shard_map/own_part/pallas_call | solution.py:27
  63.1 1.7 %collective-permute-done.12.refs_3_ = s16[8,416,128]{2,1,0:T(8,128)(2,1)} collective-permute-done((s16[8,416,128]{2,1,0:T(8,128)(2,1)}, s16[8,416,128]{2,1,0:T(8,128)(2,1)}, u32[]{:S(2)}, u32[]{:S(2)}) %collective-permute-start.12) | collective-permute-done | bytes 852000 | tf_op jit(solution)/shard_map/ppermute | solution.py:654
  64.8 3.0 %join_parts.4 = (s16[2,416,128]{2,1,0:T(8,128)(2,1)}, s16[2,416,128]{2,1,0:T(8,128)(2,1)}, s16[2,416,128]{2,1,0:T(8,128)(2,1)}, s16[2,416,128]{2,1,0:T(8,128)(2,1)}) custom-call(s32[24]{0:T(128)} %get-tuple-element.174.late, s32[24]{0:T(128)} %get-tuple-element.158.spots, bf16[24,400,128]{2,1,0:T(8,128)(2,1)S(1)} %bitcast.37, ...), custom_call_target="tpu_custom_call" | custom-call | tf_op jit(solution)/shard_map/join_parts/pallas_call | solution.py:27
  70.4 3.3 %collective-permute-done.16.refs_4_ = s16[4,416,128]{2,1,0:T(8,128)(2,1)} collective-permute-done((s16[4,416,128]{2,1,0:T(8,128)(2,1)}, s16[4,416,128]{2,1,0:T(8,128)(2,1)}, u32[]{:S(2)}, u32[]{:S(2)}) %collective-permute-start.16) | collective-permute-done | bytes 426016 | tf_op jit(solution)/shard_map/ppermute | solution.py:654
  73.7 1.4 %join_parts.5 = (s16[2,416,128]{2,1,0:T(8,128)(2,1)}, s16[2,416,128]{2,1,0:T(8,128)(2,1)}, s16[2,416,128]{2,1,0:T(8,128)(2,1)}, s16[2,416,128]{2,1,0:T(8,128)(2,1)}) custom-call(s32[24]{0:T(128)} %get-tuple-element.174.late, s32[24]{0:T(128)} %get-tuple-element.158.spots, bf16[24,400,128]{2,1,0:T(8,128)(2,1)S(1)} %bitcast.38, ...), custom_call_target="tpu_custom_call" | custom-call | tf_op jit(solution)/shard_map/join_parts/pallas_call | solution.py:27
  76.4 2.3 %collective-permute-start.19 = (s16[2,416,128]{2,1,0:T(8,128)(2,1)}, s16[2,416,128]{2,1,0:T(8,128)(2,1)}, u32[]{:S(2)}, u32[]{:S(2)}) collective-permute-start(s16[2,416,128]{2,1,0:T(8,128)(2,1)} %get-tuple-element.183), channel_id=1, source_target_pairs={{0,12},{4,8},{8,4},{12,0},{1,13},{5,9},{9,5},{13,1},{2,14},{6,10},... | collective-permute-start | bytes 638984 | tf_op jit(solution)/shard_map/ppermute | solution.py:654
  78.6 1.6 %collective-permute-start.13 = (s16[2,416,128]{2,1,0:T(8,128)(2,1)}, s16[2,416,128]{2,1,0:T(8,128)(2,1)}, u32[]{:S(2)}, u32[]{:S(2)}) collective-permute-start(s16[2,416,128]{2,1,0:T(8,128)(2,1)} %get-tuple-element.171), channel_id=1, source_target_pairs={{0,4},{4,0},{8,12},{12,8},{1,5},{5,1},{9,13},{13,9},{2,6},{6,2},{1... | collective-permute-start | bytes 638984 | tf_op jit(solution)/shard_map/ppermute | solution.py:654
  80.4 3.8 %collective-permute-done.17 = s16[2,416,128]{2,1,0:T(8,128)(2,1)} collective-permute-done((s16[2,416,128]{2,1,0:T(8,128)(2,1)}, s16[2,416,128]{2,1,0:T(8,128)(2,1)}, u32[]{:S(2)}, u32[]{:S(2)}) %collective-permute-start.17) | collective-permute-done | bytes 213024 | tf_op jit(solution)/shard_map/ppermute | solution.py:654
  84.2 2.4 %collective-permute-start.15 = (s16[2,416,128]{2,1,0:T(8,128)(2,1)}, s16[2,416,128]{2,1,0:T(8,128)(2,1)}, u32[]{:S(2)}, u32[]{:S(2)}) collective-permute-start(s16[2,416,128]{2,1,0:T(8,128)(2,1)} %get-tuple-element.173), channel_id=1, source_target_pairs={{0,12},{4,8},{8,4},{12,0},{1,13},{5,9},{9,5},{13,1},{2,14},{6,10},... | collective-permute-start | bytes 638984 | tf_op jit(solution)/shard_map/ppermute | solution.py:654
  88.0 0.8 copy.30
  88.8 0.9 pad_bitcast_fusion.occ_cols
  89.8 8.1 %update_tiles.5 = (f32[24,1,400,128]{3,2,1,0:T(8,128)}, f32[24,1,400,128]{3,2,1,0:T(8,128)}) custom-call(s32[4,128]{1,0:T(4,128)S(1)} %convert_bitcast_fusion.notes, f32[400,128]{1,0:T(8,128)S(1)} %pad_bitcast_fusion.occ_cols, f32[6,128]{1,0:T(8,128)S(1)} %copy-done.5, bf16[4,1664,128]{2,1,0:T(8,128)(2,1)} %all-to-all-done.amps, ...), custom_call_target="tpu_custom_call" | custom-call | tf_op jit(solution)/shard_map/update_tiles/pallas_call | solution.py:27
  97.8 10.1 %collective-permute-done.19 = s16[2,416,128]{2,1,0:T(8,128)(2,1)} collective-permute-done((s16[2,416,128]{2,1,0:T(8,128)(2,1)}, s16[2,416,128]{2,1,0:T(8,128)(2,1)}, u32[]{:S(2)}, u32[]{:S(2)}) %collective-permute-start.19) | collective-permute-done | bytes 213024 | tf_op jit(solution)/shard_map/ppermute | solution.py:654
  107.9 1.0 collective-permute-done.14
  108.9 8.0 %collective-permute-done.15 = s16[2,416,128]{2,1,0:T(8,128)(2,1)} collective-permute-done((s16[2,416,128]{2,1,0:T(8,128)(2,1)}, s16[2,416,128]{2,1,0:T(8,128)(2,1)}, u32[]{:S(2)}, u32[]{:S(2)}) %collective-permute-start.15) | collective-permute-done | bytes 213024 | tf_op jit(solution)/shard_map/ppermute | solution.py:654
  117.0 4.2 %conditional.3 = ((f32[24,1,400,128]{3,2,1,0:T(8,128)}, f32[24,1,400,128]{3,2,1,0:T(8,128)})) conditional(s32[]{:T(128)} %convert_element_type.26, (s32[4,128]{1,0:T(4,128)S(1)}, f32[400,128]{1,0:T(8,128)S(1)}, f32[6,128]{1,0:T(8,128)S(1)}, bf16[4,1664,128]{2,1,0:T(8,128)(2,1)}, s16[2,416,128]{2,1,0:T(8,128)(2,1)S(1)}, ...), branch_computations={%region_3.4_spmd, %region_4.5_spmd} | conditional | bytes 4915412 | solution.py:854
  117.0 4.2 %update_tiles.3 = (f32[24,1,400,128]{3,2,1,0:T(8,128)}, f32[24,1,400,128]{3,2,1,0:T(8,128)}) custom-call(s32[4,128]{1,0:T(4,128)S(1)} %get-tuple-element.81.notes, f32[400,128]{1,0:T(8,128)S(1)} %get-tuple-element.82.occ_cols, f32[6,128]{1,0:T(8,128)S(1)} %get-tuple-element.83.vir_energy, ...), custom_call_target="tpu_custom_call", output_to_operand_aliasing={{0}: (16, {}), {1}: (17, {})} | custom-call | tf_op jit(solution)/shard_map/cond/branch_0_fun/update_tiles/pallas_call | solution.py:27
  (39 shorter events, 5.2 us)
Async XLA Ops:
  0.6 15.7 %copy-start = (bf16[4,400,6,128]{3,1,2,0:T(8,128)(2,1)S(1)}, bf16[4,400,6,128]{3,1,2,0:T(8,128)(2,1)}, u32[]{:S(2)}) copy-start(bf16[4,400,6,128]{3,1,2,0:T(8,128)(2,1)} %param.14) | copy-start | bytes 7372804
  0.6 15.1 %collective-permute-start.6 = (bf16[6,128,24,128]{3,2,1,0:T(8,128)(2,1)}, bf16[6,128,24,128]{3,2,1,0:T(8,128)(2,1)}, u32[]{:S(2)}, u32[]{:S(2)}) collective-permute-start(bf16[6,128,24,128]{3,2,1,0:T(8,128)(2,1)} %ints_own.7), channel_id=1, source_target_pairs={{0,1},{1,0},{2,3},{3,2},{4,5},{5,4},{6,7},{7,6},{8,9},{9,8},{10,11... | collective-permute-start | bytes 14155784 | tf_op jit(solution)/shard_map/ppermute | solution.py:654
  0.7 15.1 %collective-permute-start.5 = (bf16[24,400,128]{2,1,0:T(8,128)(2,1)}, bf16[24,400,128]{2,1,0:T(8,128)(2,1)}, u32[]{:S(2)}, u32[]{:S(2)}) collective-permute-start(bf16[24,400,128]{2,1,0:T(8,128)(2,1)} %bitcast.30), channel_id=1, source_target_pairs={{0,1},{1,0},{2,3},{3,2},{4,5},{5,4},{6,7},{7,6},{8,9},{9,8},{10,11... | collective-permute-start | bytes 7372808 | tf_op jit(solution)/shard_map/ppermute | solution.py:654
  6.5 44.4 %all-to-all-start = ((bf16[4,1664,128]{2,1,0:T(8,128)(2,1)}), bf16[4,1664,128]{2,1,0:T(8,128)(2,1)}, u32[]{:S(2)}, u32[]{:S(2)}) async-start(bf16[4,1664,128]{2,1,0:T(8,128)(2,1)} %get-tuple-element.156), calls=%async_computation | async-start | bytes 3407872 | tf_op jit(solution)/shard_map/all_to_all | solution.py:699
  12.0 1.3 %collective-permute-start.4 = (s32[16]{0:T(128)}, s32[16]{0:T(128)S(1)}, u32[]{:S(2)}, u32[]{:S(2)}) collective-permute-start(s32[16]{0:T(128)} %get-tuple-element.161), channel_id=1, source_target_pairs={{0,1},{1,0},{2,3},{3,2},{4,5},{5,4},{6,7},{7,6},{8,9},{9,8},{10,11... | collective-permute-start | bytes 200 | tf_op jit(solution)/shard_map/ppermute | solution.py:654
  12.0 3.8 %collective-permute-start.7 = (s32[24]{0:T(128)}, s32[24]{0:T(128)S(1)}, u32[]{:S(2)}, u32[]{:S(2)}) collective-permute-start(s32[24]{0:T(128)} %get-tuple-element.177.wanted), channel_id=1, source_target_pairs={{0,2},{1,3},{2,0},{3,1},{4,6},{5,7},{6,4},{7,5},{8,10},{9,11},{10,... | collective-permute-start | bytes 296 | tf_op jit(solution)/shard_map/ppermute | solution.py:654
  13.3 2.5 %copy-start.6 = (s32[16]{0:T(128)}, s32[16]{0:T(128)S(1)}, u32[]{:S(2)}) copy-start(s32[16]{0:T(128)S(1)} %collective-permute-done.4.mask_other) | copy-start | bytes 196
  15.8 0.5 copy-start.7
  23.2 23.2 %collective-permute-start.8 = (s16[8,416,128]{2,1,0:T(8,128)(2,1)}, s16[8,416,128]{2,1,0:T(8,128)(2,1)S(1)}, u32[]{:S(2)}, u32[]{:S(2)}) collective-permute-start(s16[8,416,128]{2,1,0:T(8,128)(2,1)} %ladder_sums.2), channel_id=1, source_target_pairs={{0,2},{1,3},{2,0},{3,1},{4,6},{5,7},{6,4},{7,5},{8,10},{9,11},{10,... | collective-permute-start | bytes 2555912 | tf_op jit(solution)/shard_map/ppermute | solution.py:654
  32.9 31.9 %collective-permute-start.12 = (s16[8,416,128]{2,1,0:T(8,128)(2,1)}, s16[8,416,128]{2,1,0:T(8,128)(2,1)}, u32[]{:S(2)}, u32[]{:S(2)}) collective-permute-start(s16[8,416,128]{2,1,0:T(8,128)(2,1)} %get-tuple-element.169), channel_id=1, source_target_pairs={{0,2},{1,3},{2,0},{3,1},{4,6},{5,7},{6,4},{7,5},{8,10},{9,11},{10,... | collective-permute-start | bytes 2555912 | tf_op jit(solution)/shard_map/ppermute | solution.py:654
  34.4 39.2 %collective-permute-start.16 = (s16[4,416,128]{2,1,0:T(8,128)(2,1)}, s16[4,416,128]{2,1,0:T(8,128)(2,1)}, u32[]{:S(2)}, u32[]{:S(2)}) collective-permute-start(s16[4,416,128]{2,1,0:T(8,128)(2,1)} %get-tuple-element.175), channel_id=1, source_target_pairs={{0,2},{1,3},{2,0},{3,1},{4,6},{5,7},{6,4},{7,5},{8,10},{9,11},{10,... | collective-permute-start | bytes 1277960 | tf_op jit(solution)/shard_map/ppermute | solution.py:654
  46.4 0.9 copy-start.1
  51.8 24.6 %collective-permute-start.9 = (s16[2,416,128]{2,1,0:T(8,128)(2,1)}, s16[2,416,128]{2,1,0:T(8,128)(2,1)S(1)}, u32[]{:S(2)}, u32[]{:S(2)}) collective-permute-start(s16[2,416,128]{2,1,0:T(8,128)(2,1)} %get-tuple-element.164), channel_id=1, source_target_pairs={{0,4},{4,0},{8,12},{12,8},{1,5},{5,1},{9,13},{13,9},{2,6},{6,2},{1... | collective-permute-start | bytes 638984 | tf_op jit(solution)/shard_map/ppermute | solution.py:654
  53.0 25.6 %collective-permute-start.10 = (s16[2,416,128]{2,1,0:T(8,128)(2,1)}, s16[2,416,128]{2,1,0:T(8,128)(2,1)S(1)}, u32[]{:S(2)}, u32[]{:S(2)}) collective-permute-start(s16[2,416,128]{2,1,0:T(8,128)(2,1)} %get-tuple-element.165), channel_id=1, source_target_pairs={{0,8},{4,12},{8,0},{12,4},{1,9},{5,13},{9,1},{13,5},{2,10},{6,14},... | collective-permute-start | bytes 638984 | tf_op jit(solution)/shard_map/ppermute | solution.py:654
  55.8 24.4 %collective-permute-start.11 = (s16[2,416,128]{2,1,0:T(8,128)(2,1)}, s16[2,416,128]{2,1,0:T(8,128)(2,1)S(1)}, u32[]{:S(2)}, u32[]{:S(2)}) collective-permute-start(s16[2,416,128]{2,1,0:T(8,128)(2,1)} %get-tuple-element.166), channel_id=1, source_target_pairs={{0,12},{4,8},{8,4},{12,0},{1,13},{5,9},{9,5},{13,1},{2,14},{6,10},... | collective-permute-start | bytes 638984 | tf_op jit(solution)/shard_map/ppermute | solution.py:654
  63.1 4.7 %copy-start.8 = (s32[24]{0:T(128)S(1)}, s32[24]{0:T(128)}, u32[]{:S(2)}) copy-start(s32[24]{0:T(128)} %copy-done.7) | copy-start | bytes 292
  63.1 5.4 %copy-start.9 = (s32[24]{0:T(128)S(1)}, s32[24]{0:T(128)}, u32[]{:S(2)}) copy-start(s32[24]{0:T(128)} %get-tuple-element.177.wanted) | copy-start | bytes 292
  70.4 19.4 %copy-start.5 = (f32[6,128]{1,0:T(8,128)S(1)}, f32[6,128]{1,0:T(8,128)}, u32[]{:S(2)}) copy-start(f32[6,128]{1,0:T(8,128)} %vir_energy.1) | copy-start | bytes 9220
  75.1 9.2 %collective-permute-start.17 = (s16[2,416,128]{2,1,0:T(8,128)(2,1)}, s16[2,416,128]{2,1,0:T(8,128)(2,1)}, u32[]{:S(2)}, u32[]{:S(2)}) collective-permute-start(s16[2,416,128]{2,1,0:T(8,128)(2,1)} %get-tuple-element.181), channel_id=1, source_target_pairs={{0,4},{4,0},{8,12},{12,8},{1,5},{5,1},{9,13},{13,9},{2,6},{6,2},{1... | collective-permute-start | bytes 638984 | tf_op jit(solution)/shard_map/ppermute | solution.py:654
  75.8 22.0 %collective-permute-start.18 = (s16[2,416,128]{2,1,0:T(8,128)(2,1)}, s16[2,416,128]{2,1,0:T(8,128)(2,1)}, u32[]{:S(2)}, u32[]{:S(2)}) collective-permute-start(s16[2,416,128]{2,1,0:T(8,128)(2,1)} %get-tuple-element.182), channel_id=1, source_target_pairs={{0,8},{4,12},{8,0},{12,4},{1,9},{5,13},{9,1},{13,5},{2,10},{6,14},... | collective-permute-start | bytes 638984 | tf_op jit(solution)/shard_map/ppermute | solution.py:654
  76.4 31.6 %collective-permute-start.19 = (s16[2,416,128]{2,1,0:T(8,128)(2,1)}, s16[2,416,128]{2,1,0:T(8,128)(2,1)}, u32[]{:S(2)}, u32[]{:S(2)}) collective-permute-start(s16[2,416,128]{2,1,0:T(8,128)(2,1)} %get-tuple-element.183), channel_id=1, source_target_pairs={{0,12},{4,8},{8,4},{12,0},{1,13},{5,9},{9,5},{13,1},{2,14},{6,10},... | collective-permute-start | bytes 638984 | tf_op jit(solution)/shard_map/ppermute | solution.py:654
  78.6 29.3 %collective-permute-start.13 = (s16[2,416,128]{2,1,0:T(8,128)(2,1)}, s16[2,416,128]{2,1,0:T(8,128)(2,1)}, u32[]{:S(2)}, u32[]{:S(2)}) collective-permute-start(s16[2,416,128]{2,1,0:T(8,128)(2,1)} %get-tuple-element.171), channel_id=1, source_target_pairs={{0,4},{4,0},{8,12},{12,8},{1,5},{5,1},{9,13},{13,9},{2,6},{6,2},{1... | collective-permute-start | bytes 638984 | tf_op jit(solution)/shard_map/ppermute | solution.py:654
  80.2 28.7 %collective-permute-start.14 = (s16[2,416,128]{2,1,0:T(8,128)(2,1)}, s16[2,416,128]{2,1,0:T(8,128)(2,1)}, u32[]{:S(2)}, u32[]{:S(2)}) collective-permute-start(s16[2,416,128]{2,1,0:T(8,128)(2,1)} %get-tuple-element.172), channel_id=1, source_target_pairs={{0,8},{4,12},{8,0},{12,4},{1,9},{5,13},{9,1},{13,5},{2,10},{6,14},... | collective-permute-start | bytes 638984 | tf_op jit(solution)/shard_map/ppermute | solution.py:654
  84.2 32.7 %collective-permute-start.15 = (s16[2,416,128]{2,1,0:T(8,128)(2,1)}, s16[2,416,128]{2,1,0:T(8,128)(2,1)}, u32[]{:S(2)}, u32[]{:S(2)}) collective-permute-start(s16[2,416,128]{2,1,0:T(8,128)(2,1)} %get-tuple-element.173), channel_id=1, source_target_pairs={{0,12},{4,8},{8,4},{12,0},{1,13},{5,9},{9,5},{13,1},{2,14},{6,10},... | collective-permute-start | bytes 638984 | tf_op jit(solution)/shard_map/ppermute | solution.py:654
where the time goes:
time: 122 us; the launch traced here: 121 us
  Pallas kernels  55 us (45%)
  waiting for transfers between devices  32.9 us (27%)
  starting transfers between devices  24.4 us (20%)
  local copies, waits for them, and re-layouts  5.31 us (4%)
  between operations  2.92 us (2%)
    pallas_call x10, Pallas kernels, call(): pl.pallas_call(kernel, out_shape=out_shape, in_specs=in_specs, out_specs=...  55 us
    ppermute x16, waiting for transfers between devices, swap(): lax.ppermute(array, axis, [(i, i ^ bit) for i in range(lax.axis_size(axis...  32.9 us
    ppermute x16, starting transfers between devices, swap(): lax.ppermute(array, axis, [(i, i ^ bit) for i in range(lax.axis_size(axis...  18.9 us
    all_to_all x1, starting transfers between devices, body(): lax.all_to_all(packed, 'occ', split_axis=0, concat_axis=0, tiled=True)  5.5 us
  transfers between devices with their start and end apart: 17, of which 8 were waited for; matrix products, arithmetic and copies ran while one was open for 4% of the time, Pallas kernels for 42%

commit v1 on v0

--- a/solution.py
+++ b/solution.py
@@ -512,7 +512,7 @@
             @pl.when(chunk_of(size, slot) == chunk)
             def _(chunk=chunk, parts=parts):
                 at = slot - size.starts[chunk]
-                source = parts[s].at[at] if len(parts) > 1 else parts[0].at[s ^ me, at]
+                source = parts[-s].at[at] if len(parts) > 1 else parts[0].at[s ^ me, at]
                 pltpu.make_async_copy(source, target, sem).start()
 
     for s in range(size.dests):
@@ -790,7 +790,7 @@
             60,
         )
         if spread:
-            codes.append([joined[0]] + [swap(joined[s], "occ", s) for s in range(1, dests)])
+            codes.append([joined[0]] + [swap(joined[s], "occ", s) for s in range(dests - 1, 0, -1)])
         else:
             codes.append([lax.all_to_all(joined[0], "occ", split_axis=0, concat_axis=0, tiled=True)])
 

time: 122 us -> 121 us (level)
  the two profiles are of different devices: /device:TPU:8 before, /device:TPU:0 now
where the time goes in v1:
time: 121 us; the launch traced here: 119 us
  Pallas kernels  63.6 us (53%)
  starting transfers between devices  41.5 us (34%)
  local copies, waits for them, and re-layouts  5.31 us (4%)
  waiting for transfers between devices  4.56 us (4%)
  between operations  2.98 us (2%)
    pallas_call x10, Pallas kernels, call(): pl.pallas_call(kernel, out_shape=out_shape, in_specs=in_specs, out_specs=...  63.6 us
    ppermute x16, starting transfers between devices, swap(): lax.ppermute(array, axis, [(i, i ^ bit) for i in range(lax.axis_size(axis...  35.2 us
    all_to_all x1, starting transfers between devices, body(): lax.all_to_all(packed, 'occ', split_axis=0, concat_axis=0, tiled=True)  6.35 us
    ppermute x16, waiting for transfers between devices, swap(): lax.ppermute(array, axis, [(i, i ^ bit) for i in range(lax.axis_size(axis...  4.56 us
  transfers between devices with their start and end apart: 17, of which 3 were waited for; matrix products, arithmetic and copies ran while one was open for 4% of the time, Pallas kernels for 50%

profile of v1, /device:TPU:0, one launch (start us, length us, event | category | flops | bytes accessed | tf_op | source)
XLA Modules:
  0.0 118.7 jit_solution(17005339539819568955)
XLA Ops:
  1.2 5.3 %plan_tiles.1 = (s32[24]{0:T(128)}, s32[24]{0:T(128)}, s32[24]{0:T(128)}, s32[8]{0:T(128)S(1)}, s32[16]{0:T(128)}, /*index=5*/s32[16]{0:T(128)}, bf16[4,1664,128]{2,1,0:T(8,128)(2,1)}) custom-call(s32[4,6]{1,0:T(4,128)} %place_in.1, s32[4,6]{1,0:T(4,128)} %res_keep_in.1, s32[4,6]{1,0:T(4,128)} %amp_keep_in.1, s32[6,24]{1,0:T(8,128)} %int_keep_in.1, ...), custom_call_target="tpu_custom_call" | custom-call | tf_op jit(solution)/shard_map/plan_tiles/pallas_call | solution.py:27
  6.6 6.4 %all-to-all-start = ((bf16[4,1664,128]{2,1,0:T(8,128)(2,1)}), bf16[4,1664,128]{2,1,0:T(8,128)(2,1)}, u32[]{:S(2)}, u32[]{:S(2)}) async-start(bf16[4,1664,128]{2,1,0:T(8,128)(2,1)} %get-tuple-element.156), calls=%async_computation | async-start | bytes 3407872 | tf_op jit(solution)/shard_map/all_to_all | solution.py:699
  12.9 1.3 %collective-permute-start.7 = (s32[24]{0:T(128)}, s32[24]{0:T(128)S(1)}, u32[]{:S(2)}, u32[]{:S(2)}) collective-permute-start(s32[24]{0:T(128)} %get-tuple-element.177.wanted), channel_id=1, source_target_pairs={{0,2},{1,3},{2,0},{3,1},{4,6},{5,7},{6,4},{7,5},{8,10},{9,11},{10,... | collective-permute-start | bytes 296 | tf_op jit(solution)/shard_map/ppermute | solution.py:654
  14.2 2.5 %collective-permute-done.7.wanted = s32[24]{0:T(128)S(1)} collective-permute-done((s32[24]{0:T(128)}, s32[24]{0:T(128)S(1)}, u32[]{:S(2)}, u32[]{:S(2)}) %collective-permute-start.7) | collective-permute-done | bytes 128 | tf_op jit(solution)/shard_map/ppermute | solution.py:654
  17.2 8.3 %ladder_sums.2 = s16[8,416,128]{2,1,0:T(8,128)(2,1)} custom-call(s32[24]{0:T(128)} %copy-done.7, s32[16]{0:T(128)} %get-tuple-element.160.mask_own, s32[16]{0:T(128)} %copy-done.6, bf16[24,400,128]{2,1,0:T(8,128)(2,1)S(1)} %bitcast.32, bf16[6,128,24,128]{3,2,1,0:T(8,128)(2,1)} %ints_own.7, bf16[24,400,128]{2,1,0:T(8,128)(2,1)} %collective-permute-done.5.amps_other, ...), custom_call_target="tpu_custom_call" | custom-call | tf_op jit(solution)/shard_map/ladder_sums/pallas_call | solution.py:27
  25.5 2.7 %collective-permute-start.8 = (s16[8,416,128]{2,1,0:T(8,128)(2,1)}, s16[8,416,128]{2,1,0:T(8,128)(2,1)S(1)}, u32[]{:S(2)}, u32[]{:S(2)}) collective-permute-start(s16[8,416,128]{2,1,0:T(8,128)(2,1)} %ladder_sums.2), channel_id=1, source_target_pairs={{0,2},{1,3},{2,0},{3,1},{4,6},{5,7},{6,4},{7,5},{8,10},{9,11},{10,... | collective-permute-start | bytes 2555912 | tf_op jit(solution)/shard_map/ppermute | solution.py:654
  28.2 11.3 %ladder_sums.3 = (s16[8,416,128]{2,1,0:T(8,128)(2,1)}, s16[4,416,128]{2,1,0:T(8,128)(2,1)}, s16[4,416,128]{2,1,0:T(8,128)(2,1)}) custom-call(s32[24]{0:T(128)} %copy-done.7, s32[16]{0:T(128)} %get-tuple-element.160.mask_own, s32[16]{0:T(128)} %copy-done.6, bf16[24,400,128]{2,1,0:T(8,128)(2,1)S(1)} %bitcast.33, bf16[6,128,24,128]{3,2,1,0:T(8,128)(2,1)} %ints_own.7, ...), custom_call_target="tpu_custom_call" | custom-call | tf_op jit(solution)/shard_map/ladder_sums/pallas_call | solution.py:27
  39.6 2.0 %collective-permute-start.16 = (s16[4,416,128]{2,1,0:T(8,128)(2,1)}, s16[4,416,128]{2,1,0:T(8,128)(2,1)}, u32[]{:S(2)}, u32[]{:S(2)}) collective-permute-start(s16[4,416,128]{2,1,0:T(8,128)(2,1)} %get-tuple-element.175), channel_id=1, source_target_pairs={{0,2},{1,3},{2,0},{3,1},{4,6},{5,7},{6,4},{7,5},{8,10},{9,11},{10,... | collective-permute-start | bytes 1277960 | tf_op jit(solution)/shard_map/ppermute | solution.py:654
  41.6 10.3 %own_part.2.refs_0_ = f32[8,400,128]{2,1,0:T(8,128)} custom-call(s32[24]{0:T(128)} %get-tuple-element.177.wanted, s32[16]{0:T(128)} %get-tuple-element.160.mask_own, s32[16]{0:T(128)} %copy-done.6, bf16[24,400,128]{2,1,0:T(8,128)(2,1)S(1)} %bitcast.34, bf16[6,128,24,128]{3,2,1,0:T(8,128)(2,1)} %ints_own.7, ...), custom_call_target="tpu_custom_call" | custom-call | tf_op jit(solution)/shard_map/own_part/pallas_call | solution.py:27
  52.0 0.9 copy-done.1
  52.9 3.7 %join_parts.3 = (s16[2,416,128]{2,1,0:T(8,128)(2,1)S(1)}, s16[2,416,128]{2,1,0:T(8,128)(2,1)}, s16[2,416,128]{2,1,0:T(8,128)(2,1)}, s16[2,416,128]{2,1,0:T(8,128)(2,1)}) custom-call(s32[24]{0:T(128)} %get-tuple-element.174.late, s32[24]{0:T(128)} %get-tuple-element.158.spots, bf16[24,400,128]{2,1,0:T(8,128)(2,1)S(1)} %bitcast.35, ...), custom_call_target="tpu_custom_call" | custom-call | tf_op jit(solution)/shard_map/join_parts/pallas_call | solution.py:27
  56.5 0.9 slice.27
  57.4 2.5 %collective-permute-start.9 = (s16[2,416,128]{2,1,0:T(8,128)(2,1)}, s16[2,416,128]{2,1,0:T(8,128)(2,1)S(1)}, u32[]{:S(2)}, u32[]{:S(2)}) collective-permute-start(s16[2,416,128]{2,1,0:T(8,128)(2,1)} %get-tuple-element.164), channel_id=1, source_target_pairs={{0,12},{4,8},{8,4},{12,0},{1,13},{5,9},{9,5},{13,1},{2,14},{6,10},... | collective-permute-start | bytes 638984 | tf_op jit(solution)/shard_map/ppermute | solution.py:654
  59.9 1.9 %collective-permute-start.11 = (s16[2,416,128]{2,1,0:T(8,128)(2,1)}, s16[2,416,128]{2,1,0:T(8,128)(2,1)S(1)}, u32[]{:S(2)}, u32[]{:S(2)}) collective-permute-start(s16[2,416,128]{2,1,0:T(8,128)(2,1)} %get-tuple-element.166), channel_id=1, source_target_pairs={{0,4},{4,0},{8,12},{12,8},{1,5},{5,1},{9,13},{13,9},{2,6},{6,2},{1... | collective-permute-start | bytes 638984 | tf_op jit(solution)/shard_map/ppermute | solution.py:654
  61.9 8.4 %own_part.3.refs_1_ = f32[16,400,128]{2,1,0:T(8,128)} custom-call(s32[24]{0:T(128)} %get-tuple-element.177.wanted, s32[16]{0:T(128)} %get-tuple-element.160.mask_own, s32[16]{0:T(128)} %copy-done.6, bf16[24,400,128]{2,1,0:T(8,128)(2,1)S(1)} %bitcast.36, bf16[6,128,24,128]{3,2,1,0:T(8,128)(2,1)} %ints_own.7, ...), custom_call_target="tpu_custom_call" | custom-call | tf_op jit(solution)/shard_map/own_part/pallas_call | solution.py:27
  70.3 3.0 %join_parts.4 = (s16[2,416,128]{2,1,0:T(8,128)(2,1)}, s16[2,416,128]{2,1,0:T(8,128)(2,1)}, s16[2,416,128]{2,1,0:T(8,128)(2,1)}, s16[2,416,128]{2,1,0:T(8,128)(2,1)}) custom-call(s32[24]{0:T(128)} %get-tuple-element.174.late, s32[24]{0:T(128)} %get-tuple-element.158.spots, bf16[24,400,128]{2,1,0:T(8,128)(2,1)S(1)} %bitcast.37, ...), custom_call_target="tpu_custom_call" | custom-call | tf_op jit(solution)/shard_map/join_parts/pallas_call | solution.py:27
  73.3 0.6 slice.35
  73.9 0.6 slice.34
  75.8 1.4 %join_parts.5 = (s16[2,416,128]{2,1,0:T(8,128)(2,1)}, s16[2,416,128]{2,1,0:T(8,128)(2,1)}, s16[2,416,128]{2,1,0:T(8,128)(2,1)}, s16[2,416,128]{2,1,0:T(8,128)(2,1)}) custom-call(s32[24]{0:T(128)} %get-tuple-element.174.late, s32[24]{0:T(128)} %get-tuple-element.158.spots, bf16[24,400,128]{2,1,0:T(8,128)(2,1)S(1)} %bitcast.38, ...), custom_call_target="tpu_custom_call" | custom-call | tf_op jit(solution)/shard_map/join_parts/pallas_call | solution.py:27
  77.2 4.4 %collective-permute-start.17 = (s16[2,416,128]{2,1,0:T(8,128)(2,1)}, s16[2,416,128]{2,1,0:T(8,128)(2,1)}, u32[]{:S(2)}, u32[]{:S(2)}) collective-permute-start(s16[2,416,128]{2,1,0:T(8,128)(2,1)} %get-tuple-element.181), channel_id=1, source_target_pairs={{0,12},{4,8},{8,4},{12,0},{1,13},{5,9},{9,5},{13,1},{2,14},{6,10},... | collective-permute-start | bytes 638984 | tf_op jit(solution)/shard_map/ppermute | solution.py:654
  81.6 1.9 %collective-permute-start.18 = (s16[2,416,128]{2,1,0:T(8,128)(2,1)}, s16[2,416,128]{2,1,0:T(8,128)(2,1)}, u32[]{:S(2)}, u32[]{:S(2)}) collective-permute-start(s16[2,416,128]{2,1,0:T(8,128)(2,1)} %get-tuple-element.182), channel_id=1, source_target_pairs={{0,8},{4,12},{8,0},{12,4},{1,9},{5,13},{9,1},{13,5},{2,10},{6,14},... | collective-permute-start | bytes 638984 | tf_op jit(solution)/shard_map/ppermute | solution.py:654
  83.5 2.4 %collective-permute-start.13 = (s16[2,416,128]{2,1,0:T(8,128)(2,1)}, s16[2,416,128]{2,1,0:T(8,128)(2,1)}, u32[]{:S(2)}, u32[]{:S(2)}) collective-permute-start(s16[2,416,128]{2,1,0:T(8,128)(2,1)} %get-tuple-element.171), channel_id=1, source_target_pairs={{0,12},{4,8},{8,4},{12,0},{1,13},{5,9},{9,5},{13,1},{2,14},{6,10},... | collective-permute-start | bytes 638984 | tf_op jit(solution)/shard_map/ppermute | solution.py:654
  86.0 1.0 collective-permute-start.14
  87.0 1.0 collective-permute-done.17
  88.0 14.3 %collective-permute-start.15 = (s16[2,416,128]{2,1,0:T(8,128)(2,1)}, s16[2,416,128]{2,1,0:T(8,128)(2,1)}, u32[]{:S(2)}, u32[]{:S(2)}) collective-permute-start(s16[2,416,128]{2,1,0:T(8,128)(2,1)} %get-tuple-element.173), channel_id=1, source_target_pairs={{0,4},{4,0},{8,12},{12,8},{1,5},{5,1},{9,13},{13,9},{2,6},{6,2},{1... | collective-permute-start | bytes 638984 | tf_op jit(solution)/shard_map/ppermute | solution.py:654
  102.3 0.7 slice_reduce_fusion
  103.7 0.8 copy.30
  104.5 0.9 pad_bitcast_fusion.occ_cols
  105.4 8.1 %update_tiles.5 = (f32[24,1,400,128]{3,2,1,0:T(8,128)}, f32[24,1,400,128]{3,2,1,0:T(8,128)}) custom-call(s32[4,128]{1,0:T(4,128)S(1)} %convert_bitcast_fusion.notes, f32[400,128]{1,0:T(8,128)S(1)} %pad_bitcast_fusion.occ_cols, f32[6,128]{1,0:T(8,128)S(1)} %copy-done.5, bf16[4,1664,128]{2,1,0:T(8,128)(2,1)} %all-to-all-done.amps, ...), custom_call_target="tpu_custom_call" | custom-call | tf_op jit(solution)/shard_map/update_tiles/pallas_call | solution.py:27
  113.6 1.1 collective-permute-done.14
  114.7 3.9 %conditional.3 = ((f32[24,1,400,128]{3,2,1,0:T(8,128)}, f32[24,1,400,128]{3,2,1,0:T(8,128)})) conditional(s32[]{:T(128)} %convert_element_type.26, (s32[4,128]{1,0:T(4,128)S(1)}, f32[400,128]{1,0:T(8,128)S(1)}, f32[6,128]{1,0:T(8,128)S(1)}, bf16[4,1664,128]{2,1,0:T(8,128)(2,1)}, s16[2,416,128]{2,1,0:T(8,128)(2,1)S(1)}, ...), branch_computations={%region_3.4_spmd, %region_4.5_spmd} | conditional | bytes 4915412 | solution.py:854
  114.7 3.8 %update_tiles.3 = (f32[24,1,400,128]{3,2,1,0:T(8,128)}, f32[24,1,400,128]{3,2,1,0:T(8,128)}) custom-call(s32[4,128]{1,0:T(4,128)S(1)} %get-tuple-element.81.notes, f32[400,128]{1,0:T(8,128)S(1)} %get-tuple-element.82.occ_cols, f32[6,128]{1,0:T(8,128)S(1)} %get-tuple-element.83.vir_energy, ...), custom_call_target="tpu_custom_call", output_to_operand_aliasing={{0}: (16, {}), {1}: (17, {})} | custom-call | tf_op jit(solution)/shard_map/cond/branch_0_fun/update_tiles/pallas_call | solution.py:27
  (39 shorter events, 1.3 us)
Async XLA Ops:
  0.6 16.6 %copy-start = (bf16[4,400,6,128]{3,1,2,0:T(8,128)(2,1)S(1)}, bf16[4,400,6,128]{3,1,2,0:T(8,128)(2,1)}, u32[]{:S(2)}) copy-start(bf16[4,400,6,128]{3,1,2,0:T(8,128)(2,1)} %param.14) | copy-start | bytes 7372804
  0.6 16.0 %collective-permute-start.6 = (bf16[6,128,24,128]{3,2,1,0:T(8,128)(2,1)}, bf16[6,128,24,128]{3,2,1,0:T(8,128)(2,1)}, u32[]{:S(2)}, u32[]{:S(2)}) collective-permute-start(bf16[6,128,24,128]{3,2,1,0:T(8,128)(2,1)} %ints_own.7), channel_id=1, source_target_pairs={{0,1},{1,0},{2,3},{3,2},{4,5},{5,4},{6,7},{7,6},{8,9},{9,8},{10,11... | collective-permute-start | bytes 14155784 | tf_op jit(solution)/shard_map/ppermute | solution.py:654
  1.2 15.5 %collective-permute-start.5 = (bf16[24,400,128]{2,1,0:T(8,128)(2,1)}, bf16[24,400,128]{2,1,0:T(8,128)(2,1)}, u32[]{:S(2)}, u32[]{:S(2)}) collective-permute-start(bf16[24,400,128]{2,1,0:T(8,128)(2,1)} %bitcast.30), channel_id=1, source_target_pairs={{0,1},{1,0},{2,3},{3,2},{4,5},{5,4},{6,7},{7,6},{8,9},{9,8},{10,11... | collective-permute-start | bytes 7372808 | tf_op jit(solution)/shard_map/ppermute | solution.py:654
  6.6 50.0 %all-to-all-start = ((bf16[4,1664,128]{2,1,0:T(8,128)(2,1)}), bf16[4,1664,128]{2,1,0:T(8,128)(2,1)}, u32[]{:S(2)}, u32[]{:S(2)}) async-start(bf16[4,1664,128]{2,1,0:T(8,128)(2,1)} %get-tuple-element.156), calls=%async_computation | async-start | bytes 3407872 | tf_op jit(solution)/shard_map/all_to_all | solution.py:699
  12.9 1.3 %collective-permute-start.4 = (s32[16]{0:T(128)}, s32[16]{0:T(128)S(1)}, u32[]{:S(2)}, u32[]{:S(2)}) collective-permute-start(s32[16]{0:T(128)} %get-tuple-element.161), channel_id=1, source_target_pairs={{0,1},{1,0},{2,3},{3,2},{4,5},{5,4},{6,7},{7,6},{8,9},{9,8},{10,11... | collective-permute-start | bytes 200 | tf_op jit(solution)/shard_map/ppermute | solution.py:654
  12.9 3.8 %collective-permute-start.7 = (s32[24]{0:T(128)}, s32[24]{0:T(128)S(1)}, u32[]{:S(2)}, u32[]{:S(2)}) collective-permute-start(s32[24]{0:T(128)} %get-tuple-element.177.wanted), channel_id=1, source_target_pairs={{0,2},{1,3},{2,0},{3,1},{4,6},{5,7},{6,4},{7,5},{8,10},{9,11},{10,... | collective-permute-start | bytes 296 | tf_op jit(solution)/shard_map/ppermute | solution.py:654
  14.2 2.5 %copy-start.6 = (s32[16]{0:T(128)}, s32[16]{0:T(128)S(1)}, u32[]{:S(2)}) copy-start(s32[16]{0:T(128)S(1)} %collective-permute-done.4.mask_other) | copy-start | bytes 196
  16.7 0.5 copy-start.7
  25.5 26.4 %collective-permute-start.8 = (s16[8,416,128]{2,1,0:T(8,128)(2,1)}, s16[8,416,128]{2,1,0:T(8,128)(2,1)S(1)}, u32[]{:S(2)}, u32[]{:S(2)}) collective-permute-start(s16[8,416,128]{2,1,0:T(8,128)(2,1)} %ladder_sums.2), channel_id=1, source_target_pairs={{0,2},{1,3},{2,0},{3,1},{4,6},{5,7},{6,4},{7,5},{8,10},{9,11},{10,... | collective-permute-start | bytes 2555912 | tf_op jit(solution)/shard_map/ppermute | solution.py:654
  39.5 30.7 %collective-permute-start.12 = (s16[8,416,128]{2,1,0:T(8,128)(2,1)}, s16[8,416,128]{2,1,0:T(8,128)(2,1)}, u32[]{:S(2)}, u32[]{:S(2)}) collective-permute-start(s16[8,416,128]{2,1,0:T(8,128)(2,1)} %get-tuple-element.169), channel_id=1, source_target_pairs={{0,2},{1,3},{2,0},{3,1},{4,6},{5,7},{6,4},{7,5},{8,10},{9,11},{10,... | collective-permute-start | bytes 2555912 | tf_op jit(solution)/shard_map/ppermute | solution.py:654
  39.6 36.2 %collective-permute-start.16 = (s16[4,416,128]{2,1,0:T(8,128)(2,1)}, s16[4,416,128]{2,1,0:T(8,128)(2,1)}, u32[]{:S(2)}, u32[]{:S(2)}) collective-permute-start(s16[4,416,128]{2,1,0:T(8,128)(2,1)} %get-tuple-element.175), channel_id=1, source_target_pairs={{0,2},{1,3},{2,0},{3,1},{4,6},{5,7},{6,4},{7,5},{8,10},{9,11},{10,... | collective-permute-start | bytes 1277960 | tf_op jit(solution)/shard_map/ppermute | solution.py:654
  51.9 0.9 copy-start.1
  57.4 26.1 %collective-permute-start.9 = (s16[2,416,128]{2,1,0:T(8,128)(2,1)}, s16[2,416,128]{2,1,0:T(8,128)(2,1)S(1)}, u32[]{:S(2)}, u32[]{:S(2)}) collective-permute-start(s16[2,416,128]{2,1,0:T(8,128)(2,1)} %get-tuple-element.164), channel_id=1, source_target_pairs={{0,12},{4,8},{8,4},{12,0},{1,13},{5,9},{9,5},{13,1},{2,14},{6,10},... | collective-permute-start | bytes 638984 | tf_op jit(solution)/shard_map/ppermute | solution.py:654
  59.9 23.6 %collective-permute-start.10 = (s16[2,416,128]{2,1,0:T(8,128)(2,1)}, s16[2,416,128]{2,1,0:T(8,128)(2,1)S(1)}, u32[]{:S(2)}, u32[]{:S(2)}) collective-permute-start(s16[2,416,128]{2,1,0:T(8,128)(2,1)} %get-tuple-element.165), channel_id=1, source_target_pairs={{0,8},{4,12},{8,0},{12,4},{1,9},{5,13},{9,1},{13,5},{2,10},{6,14},... | collective-permute-start | bytes 638984 | tf_op jit(solution)/shard_map/ppermute | solution.py:654
  59.9 26.1 %collective-permute-start.11 = (s16[2,416,128]{2,1,0:T(8,128)(2,1)}, s16[2,416,128]{2,1,0:T(8,128)(2,1)S(1)}, u32[]{:S(2)}, u32[]{:S(2)}) collective-permute-start(s16[2,416,128]{2,1,0:T(8,128)(2,1)} %get-tuple-element.166), channel_id=1, source_target_pairs={{0,4},{4,0},{8,12},{12,8},{1,5},{5,1},{9,13},{13,9},{2,6},{6,2},{1... | collective-permute-start | bytes 638984 | tf_op jit(solution)/shard_map/ppermute | solution.py:654
  70.2 3.0 %copy-start.8 = (s32[24]{0:T(128)S(1)}, s32[24]{0:T(128)}, u32[]{:S(2)}) copy-start(s32[24]{0:T(128)} %copy-done.7) | copy-start | bytes 292
  70.2 3.7 %copy-start.9 = (s32[24]{0:T(128)S(1)}, s32[24]{0:T(128)}, u32[]{:S(2)}) copy-start(s32[24]{0:T(128)} %get-tuple-element.177.wanted) | copy-start | bytes 292
  75.8 29.6 %copy-start.5 = (f32[6,128]{1,0:T(8,128)S(1)}, f32[6,128]{1,0:T(8,128)}, u32[]{:S(2)}) copy-start(f32[6,128]{1,0:T(8,128)} %vir_energy.1) | copy-start | bytes 9220
  77.2 10.8 %collective-permute-start.17 = (s16[2,416,128]{2,1,0:T(8,128)(2,1)}, s16[2,416,128]{2,1,0:T(8,128)(2,1)}, u32[]{:S(2)}, u32[]{:S(2)}) collective-permute-start(s16[2,416,128]{2,1,0:T(8,128)(2,1)} %get-tuple-element.181), channel_id=1, source_target_pairs={{0,12},{4,8},{8,4},{12,0},{1,13},{5,9},{9,5},{13,1},{2,14},{6,10},... | collective-permute-start | bytes 638984 | tf_op jit(solution)/shard_map/ppermute | solution.py:654
  81.6 32.0 %collective-permute-start.18 = (s16[2,416,128]{2,1,0:T(8,128)(2,1)}, s16[2,416,128]{2,1,0:T(8,128)(2,1)}, u32[]{:S(2)}, u32[]{:S(2)}) collective-permute-start(s16[2,416,128]{2,1,0:T(8,128)(2,1)} %get-tuple-element.182), channel_id=1, source_target_pairs={{0,8},{4,12},{8,0},{12,4},{1,9},{5,13},{9,1},{13,5},{2,10},{6,14},... | collective-permute-start | bytes 638984 | tf_op jit(solution)/shard_map/ppermute | solution.py:654
  83.5 30.1 %collective-permute-start.19 = (s16[2,416,128]{2,1,0:T(8,128)(2,1)}, s16[2,416,128]{2,1,0:T(8,128)(2,1)}, u32[]{:S(2)}, u32[]{:S(2)}) collective-permute-start(s16[2,416,128]{2,1,0:T(8,128)(2,1)} %get-tuple-element.183), channel_id=1, source_target_pairs={{0,4},{4,0},{8,12},{12,8},{1,5},{5,1},{9,13},{13,9},{2,6},{6,2},{1... | collective-permute-start | bytes 638984 | tf_op jit(solution)/shard_map/ppermute | solution.py:654
  83.5 30.0 %collective-permute-start.13 = (s16[2,416,128]{2,1,0:T(8,128)(2,1)}, s16[2,416,128]{2,1,0:T(8,128)(2,1)}, u32[]{:S(2)}, u32[]{:S(2)}) collective-permute-start(s16[2,416,128]{2,1,0:T(8,128)(2,1)} %get-tuple-element.171), channel_id=1, source_target_pairs={{0,12},{4,8},{8,4},{12,0},{1,13},{5,9},{9,5},{13,1},{2,14},{6,10},... | collective-permute-start | bytes 638984 | tf_op jit(solution)/shard_map/ppermute | solution.py:654
  86.0 28.7 %collective-permute-start.14 = (s16[2,416,128]{2,1,0:T(8,128)(2,1)}, s16[2,416,128]{2,1,0:T(8,128)(2,1)}, u32[]{:S(2)}, u32[]{:S(2)}) collective-permute-start(s16[2,416,128]{2,1,0:T(8,128)(2,1)} %get-tuple-element.172), channel_id=1, source_target_pairs={{0,8},{4,12},{8,0},{12,4},{1,9},{5,13},{9,1},{13,5},{2,10},{6,14},... | collective-permute-start | bytes 638984 | tf_op jit(solution)/shard_map/ppermute | solution.py:654
  88.0 26.7 %collective-permute-start.15 = (s16[2,416,128]{2,1,0:T(8,128)(2,1)}, s16[2,416,128]{2,1,0:T(8,128)(2,1)}, u32[]{:S(2)}, u32[]{:S(2)}) collective-permute-start(s16[2,416,128]{2,1,0:T(8,128)(2,1)} %get-tuple-element.173), channel_id=1, source_target_pairs={{0,4},{4,0},{8,12},{12,8},{1,5},{5,1},{9,13},{13,9},{2,6},{6,2},{1... | collective-permute-start | bytes 638984 | tf_op jit(solution)/shard_map/ppermute | solution.py:654

commit v2 on v1

--- a/solution.py
+++ b/solution.py
@@ -751,6 +751,12 @@
     own_spans = [pieces[0]] + ([(pieces[0][1], tiles)] if len(pieces) > 1 else [])
     own = [own_part(own_spans[0], wanted)]
 
+    beyond = []
+    if rare:
+        for theirs in wanted_other:
+            mine, theirs, _ = lax.optimization_barrier((wanted, theirs, own[0]))
+            beyond.append(jnp.max(jnp.maximum(mine, theirs)[pieces[-1][0] :]) >= 0)
+
     codes = []
     for c in range(chunks):
         use = pieces if c == chunks - 1 else pieces[: min(c + 1, len(pieces))]
@@ -758,10 +764,9 @@
         per_chunk = per_dest * dests
         if rare and c == chunks - 1:
             for k in range(1, runs):
-                part, mine, theirs, _ = lax.optimization_barrier((sums_came[k - 1][-1], wanted, wanted_other[k - 1], joined[0]))
-                beyond = (mine[use[-1][0]] >= 0) | (theirs[use[-1][0]] >= 0)
+                part, _ = lax.optimization_barrier((sums_came[k - 1][-1], joined[0]))
                 sums_came[k - 1][-1] = lax.cond(
-                    beyond, functools.partial(swap, axis="vir", bit=2 * k), lambda part: part, part
+                    beyond[k - 1], functools.partial(swap, axis="vir", bit=2 * k), lambda part: part, part
                 )
         came = [part for parts in sums_came for part in parts[: len(use)]]
         if codes:

time: 121 us -> 122 us (level)
  starting transfers between devices: 41.5 us -> 31.8 us
  waiting for transfers between devices: 4.56 us -> 10.3 us
  Pallas kernels: 63.6 us -> 66.5 us
  other arithmetic: 0.72 us -> 2.95 us
    ppermute x16, starting transfers between devices: 35.2 us -> 25.7 us  [swap(): lax.ppermute(array, axis, [(i, i ^ bit) for i in range(lax.axis_size(axis...]
    ppermute x16, waiting for transfers between devices: 4.56 us -> 10.3 us  [swap(): lax.ppermute(array, axis, [(i, i ^ bit) for i in range(lax.axis_size(axis...]
    pallas_call x10, Pallas kernels: 63.6 us -> 66.5 us  [call(): pl.pallas_call(kernel, out_shape=out_shape, in_specs=in_specs, out_specs=...]
    slice x2 -> x0, local copies, waits for them, and re-layouts: 1.24 us -> none  [body(): beyond = (mine[use[-1][0]] >= 0) | (theirs[use[-1][0]] >= 0)]
    unnamed x15 -> x17, local copies, waits for them, and re-layouts: 2.25 us -> 3.08 us
  transfers between devices with their start and end apart: 17 -> 17, of which waited for: 3 -> 3; matrix products, arithmetic and copies ran while one was open for 4% -> 6% of each run, Pallas kernels for 50% -> 52%
where the time goes in v2:
time: 122 us; the launch traced here: 120 us
  Pallas kernels  66.5 us (55%)
  starting transfers between devices  31.8 us (26%)
  waiting for transfers between devices  10.3 us (8%)
  local copies, waits for them, and re-layouts  6.07 us (5%)
  other arithmetic  2.95 us (2%)
  between operations  2.36 us (2%)
    pallas_call x10, Pallas kernels, call(): pl.pallas_call(kernel, out_shape=out_shape, in_specs=in_specs, out_specs=...  66.5 us
    ppermute x16, starting transfers between devices, swap(): lax.ppermute(array, axis, [(i, i ^ bit) for i in range(lax.axis_size(axis...  25.7 us
    ppermute x16, waiting for transfers between devices, swap(): lax.ppermute(array, axis, [(i, i ^ bit) for i in range(lax.axis_size(axis...  10.3 us
    all_to_all x1, starting transfers between devices, body(): lax.all_to_all(packed, 'occ', split_axis=0, concat_axis=0, tiled=True)  6.12 us
    unnamed x17, local copies, waits for them, and re-layouts  3.08 us
  transfers between devices with their start and end apart: 17, of which 3 were waited for; matrix products, arithmetic and copies ran while one was open for 6% of the time, Pallas kernels for 52%

profile of v2, /device:TPU:0, one launch (start us, length us, event | category | flops | bytes accessed | tf_op | source)
XLA Modules:
  0.0 120.0 jit_solution(15975260069705248556)
XLA Ops:
  1.2 5.3 %plan_tiles.1 = (s32[24]{0:T(128)}, s32[24]{0:T(128)}, s32[24]{0:T(128)}, s32[8]{0:T(128)}, s32[16]{0:T(128)}, /*index=5*/s32[16]{0:T(128)}, bf16[4,1664,128]{2,1,0:T(8,128)(2,1)}) custom-call(s32[4,6]{1,0:T(4,128)} %place_in.1, s32[4,6]{1,0:T(4,128)} %res_keep_in.1, s32[4,6]{1,0:T(4,128)} %amp_keep_in.1, s32[6,24]{1,0:T(8,128)} %int_keep_in.1, ...), custom_call_target="tpu_custom_call" | custom-call | tf_op jit(solution)/shard_map/plan_tiles/pallas_call | solution.py:27
  6.6 6.1 %all-to-all-start = ((bf16[4,1664,128]{2,1,0:T(8,128)(2,1)}), bf16[4,1664,128]{2,1,0:T(8,128)(2,1)}, u32[]{:S(2)}, u32[]{:S(2)}) async-start(bf16[4,1664,128]{2,1,0:T(8,128)(2,1)} %get-tuple-element.156), calls=%async_computation | async-start | bytes 3407872 | tf_op jit(solution)/shard_map/all_to_all | solution.py:699
  12.7 1.8 %collective-permute-start.7 = (s32[24]{0:T(128)}, s32[24]{0:T(128)S(1)}, u32[]{:S(2)}, u32[]{:S(2)}) collective-permute-start(s32[24]{0:T(128)} %get-tuple-element.176.wanted), channel_id=1, source_target_pairs={{0,2},{1,3},{2,0},{3,1},{4,6},{5,7},{6,4},{7,5},{8,10},{9,11},{10,... | collective-permute-start | bytes 296 | tf_op jit(solution)/shard_map/ppermute | solution.py:654
  14.5 2.0 %collective-permute-done.7.wanted = s32[24]{0:T(128)S(1)} collective-permute-done((s32[24]{0:T(128)}, s32[24]{0:T(128)S(1)}, u32[]{:S(2)}, u32[]{:S(2)}) %collective-permute-start.7) | collective-permute-done | bytes 128 | tf_op jit(solution)/shard_map/ppermute | solution.py:654
  17.1 8.8 %ladder_sums.2 = s16[8,416,128]{2,1,0:T(8,128)(2,1)} custom-call(s32[24]{0:T(128)} %copy-done.8, s32[16]{0:T(128)} %get-tuple-element.160.mask_own, s32[16]{0:T(128)} %copy-done.6, bf16[24,400,128]{2,1,0:T(8,128)(2,1)S(1)} %bitcast.31, bf16[6,128,24,128]{3,2,1,0:T(8,128)(2,1)} %ints_own.7, bf16[24,400,128]{2,1,0:T(8,128)(2,1)} %collective-permute-done.5.amps_other, ...), custom_call_target="tpu_custom_call" | custom-call | tf_op jit(solution)/shard_map/ladder_sums/pallas_call | solution.py:27
  25.9 1.5 %collective-permute-start.8 = (s16[8,416,128]{2,1,0:T(8,128)(2,1)}, s16[8,416,128]{2,1,0:T(8,128)(2,1)S(1)}, u32[]{:S(2)}, u32[]{:S(2)}) collective-permute-start(s16[8,416,128]{2,1,0:T(8,128)(2,1)} %ladder_sums.2), channel_id=1, source_target_pairs={{0,2},{1,3},{2,0},{3,1},{4,6},{5,7},{6,4},{7,5},{8,10},{9,11},{10,... | collective-permute-start | bytes 2555912 | tf_op jit(solution)/shard_map/ppermute | solution.py:654
  27.4 7.9 %ladder_sums.3 = (s16[8,416,128]{2,1,0:T(8,128)(2,1)}, s16[4,416,128]{2,1,0:T(8,128)(2,1)}, s16[4,416,128]{2,1,0:T(8,128)(2,1)}) custom-call(s32[24]{0:T(128)} %copy-done.8, s32[16]{0:T(128)} %get-tuple-element.160.mask_own, s32[16]{0:T(128)} %copy-done.6, bf16[24,400,128]{2,1,0:T(8,128)(2,1)S(1)} %bitcast.32, bf16[6,128,24,128]{3,2,1,0:T(8,128)(2,1)} %ints_own.7, ...), custom_call_target="tpu_custom_call" | custom-call | tf_op jit(solution)/shard_map/ladder_sums/pallas_call | solution.py:27
  35.4 1.2 %collective-permute-start.12 = (s16[8,416,128]{2,1,0:T(8,128)(2,1)}, s16[8,416,128]{2,1,0:T(8,128)(2,1)}, u32[]{:S(2)}, u32[]{:S(2)}) collective-permute-start(s16[8,416,128]{2,1,0:T(8,128)(2,1)} %get-tuple-element.169), channel_id=1, source_target_pairs={{0,2},{1,3},{2,0},{3,1},{4,6},{5,7},{6,4},{7,5},{8,10},{9,11},{10,... | collective-permute-start | bytes 2555912 | tf_op jit(solution)/shard_map/ppermute | solution.py:654
  36.6 0.9 collective-permute-start.16
  37.5 11.1 %own_part.2.refs_0_ = f32[8,400,128]{2,1,0:T(8,128)} custom-call(s32[24]{0:T(128)} %get-tuple-element.176.wanted, s32[16]{0:T(128)} %get-tuple-element.160.mask_own, s32[16]{0:T(128)} %copy-done.6, bf16[24,400,128]{2,1,0:T(8,128)(2,1)S(1)} %bitcast.33, bf16[6,128,24,128]{3,2,1,0:T(8,128)(2,1)} %ints_own.7, ...), custom_call_target="tpu_custom_call" | custom-call | tf_op jit(solution)/shard_map/own_part/pallas_call | solution.py:27
  48.5 0.8 slice_reduce_fusion.1
  50.0 0.9 copy-done.1
  51.0 3.8 %join_parts.3 = (s16[2,416,128]{2,1,0:T(8,128)(2,1)S(1)}, s16[2,416,128]{2,1,0:T(8,128)(2,1)}, s16[2,416,128]{2,1,0:T(8,128)(2,1)}, s16[2,416,128]{2,1,0:T(8,128)(2,1)}) custom-call(s32[24]{0:T(128)} %get-tuple-element.174.late, s32[24]{0:T(128)} %get-tuple-element.158.spots, bf16[24,400,128]{2,1,0:T(8,128)(2,1)S(1)} %bitcast.34, ...), custom_call_target="tpu_custom_call" | custom-call | tf_op jit(solution)/shard_map/join_parts/pallas_call | solution.py:27
  54.7 0.9 slice.24
  56.8 2.8 %collective-permute-start.9 = (s16[2,416,128]{2,1,0:T(8,128)(2,1)}, s16[2,416,128]{2,1,0:T(8,128)(2,1)S(1)}, u32[]{:S(2)}, u32[]{:S(2)}) collective-permute-start(s16[2,416,128]{2,1,0:T(8,128)(2,1)} %get-tuple-element.164), channel_id=1, source_target_pairs={{0,12},{4,8},{8,4},{12,0},{1,13},{5,9},{9,5},{13,1},{2,14},{6,10},... | collective-permute-start | bytes 638984 | tf_op jit(solution)/shard_map/ppermute | solution.py:654
  59.6 1.5 %collective-permute-start.10 = (s16[2,416,128]{2,1,0:T(8,128)(2,1)}, s16[2,416,128]{2,1,0:T(8,128)(2,1)S(1)}, u32[]{:S(2)}, u32[]{:S(2)}) collective-permute-start(s16[2,416,128]{2,1,0:T(8,128)(2,1)} %get-tuple-element.165), channel_id=1, source_target_pairs={{0,8},{4,12},{8,0},{12,4},{1,9},{5,13},{9,1},{13,5},{2,10},{6,14},... | collective-permute-start | bytes 638984 | tf_op jit(solution)/shard_map/ppermute | solution.py:654
  61.2 11.1 %own_part.3.refs_1_ = f32[16,400,128]{2,1,0:T(8,128)} custom-call(s32[24]{0:T(128)} %get-tuple-element.176.wanted, s32[16]{0:T(128)} %get-tuple-element.160.mask_own, s32[16]{0:T(128)} %copy-done.6, bf16[24,400,128]{2,1,0:T(8,128)(2,1)S(1)} %bitcast.35, bf16[6,128,24,128]{3,2,1,0:T(8,128)(2,1)} %ints_own.7, ...), custom_call_target="tpu_custom_call" | custom-call | tf_op jit(solution)/shard_map/own_part/pallas_call | solution.py:27
  72.3 3.2 %join_parts.4 = (s16[2,416,128]{2,1,0:T(8,128)(2,1)S(1)}, s16[2,416,128]{2,1,0:T(8,128)(2,1)}, s16[2,416,128]{2,1,0:T(8,128)(2,1)}, s16[2,416,128]{2,1,0:T(8,128)(2,1)}) custom-call(s32[24]{0:T(128)} %get-tuple-element.174.late, s32[24]{0:T(128)} %get-tuple-element.158.spots, bf16[24,400,128]{2,1,0:T(8,128)(2,1)S(1)} %bitcast.36, ...), custom_call_target="tpu_custom_call" | custom-call | tf_op jit(solution)/shard_map/join_parts/pallas_call | solution.py:27
  75.6 0.8 fusion
  76.4 2.8 %join_parts.5 = (s16[2,416,128]{2,1,0:T(8,128)(2,1)}, s16[2,416,128]{2,1,0:T(8,128)(2,1)}, s16[2,416,128]{2,1,0:T(8,128)(2,1)}, s16[2,416,128]{2,1,0:T(8,128)(2,1)}) custom-call(s32[24]{0:T(128)} %get-tuple-element.174.late, s32[24]{0:T(128)} %get-tuple-element.158.spots, bf16[24,400,128]{2,1,0:T(8,128)(2,1)S(1)} %bitcast.37, ...), custom_call_target="tpu_custom_call" | custom-call | tf_op jit(solution)/shard_map/join_parts/pallas_call | solution.py:27
  79.3 1.2 collective-permute-start.18
  80.5 3.2 %collective-permute-start.19 = (s16[2,416,128]{2,1,0:T(8,128)(2,1)}, s16[2,416,128]{2,1,0:T(8,128)(2,1)}, u32[]{:S(2)}, u32[]{:S(2)}) collective-permute-start(s16[2,416,128]{2,1,0:T(8,128)(2,1)} %get-tuple-element.183), channel_id=1, source_target_pairs={{0,4},{4,0},{8,12},{12,8},{1,5},{5,1},{9,13},{13,9},{2,6},{6,2},{1... | collective-permute-start | bytes 638984 | tf_op jit(solution)/shard_map/ppermute | solution.py:654
  83.9 1.5 %collective-permute-start.14 = (s16[2,416,128]{2,1,0:T(8,128)(2,1)}, s16[2,416,128]{2,1,0:T(8,128)(2,1)}, u32[]{:S(2)}, u32[]{:S(2)}) collective-permute-start(s16[2,416,128]{2,1,0:T(8,128)(2,1)} %get-tuple-element.172), channel_id=1, source_target_pairs={{0,8},{4,12},{8,0},{12,4},{1,9},{5,13},{9,1},{13,5},{2,10},{6,14},... | collective-permute-start | bytes 638984 | tf_op jit(solution)/shard_map/ppermute | solution.py:654
  85.3 4.4 %collective-permute-done.17 = s16[2,416,128]{2,1,0:T(8,128)(2,1)} collective-permute-done((s16[2,416,128]{2,1,0:T(8,128)(2,1)}, s16[2,416,128]{2,1,0:T(8,128)(2,1)}, u32[]{:S(2)}, u32[]{:S(2)}) %collective-permute-start.17) | collective-permute-done | bytes 213024 | tf_op jit(solution)/shard_map/ppermute | solution.py:654
  89.7 9.2 %collective-permute-start.15 = (s16[2,416,128]{2,1,0:T(8,128)(2,1)}, s16[2,416,128]{2,1,0:T(8,128)(2,1)}, u32[]{:S(2)}, u32[]{:S(2)}) collective-permute-start(s16[2,416,128]{2,1,0:T(8,128)(2,1)} %get-tuple-element.173), channel_id=1, source_target_pairs={{0,4},{4,0},{8,12},{12,8},{1,5},{5,1},{9,13},{13,9},{2,6},{6,2},{1... | collective-permute-start | bytes 638984 | tf_op jit(solution)/shard_map/ppermute | solution.py:654
  98.9 0.7 slice_reduce_fusion
  100.9 1.6 %copy.30 = f32[16,400]{0,1:T(8,128)} copy(f32[16,400]{1,0:T(8,128)} %bitcast.41) | data formatting | bytes 51200
  102.5 0.9 pad_bitcast_fusion.occ_cols
  103.4 8.4 %update_tiles.5 = (f32[24,1,400,128]{3,2,1,0:T(8,128)}, f32[24,1,400,128]{3,2,1,0:T(8,128)}) custom-call(s32[4,128]{1,0:T(4,128)} %copy-done.5, f32[400,128]{1,0:T(8,128)S(1)} %pad_bitcast_fusion.occ_cols, f32[6,128]{1,0:T(8,128)} %vir_energy.1, bf16[4,1664,128]{2,1,0:T(8,128)(2,1)} %all-to-all-done.amps, ...), custom_call_target="tpu_custom_call" | custom-call | tf_op jit(solution)/shard_map/update_tiles/pallas_call | solution.py:27
  111.8 3.9 %collective-permute-done.14 = s16[2,416,128]{2,1,0:T(8,128)(2,1)} collective-permute-done((s16[2,416,128]{2,1,0:T(8,128)(2,1)}, s16[2,416,128]{2,1,0:T(8,128)(2,1)}, u32[]{:S(2)}, u32[]{:S(2)}) %collective-permute-start.14) | collective-permute-done | bytes 213024 | tf_op jit(solution)/shard_map/ppermute | solution.py:654
  115.8 4.1 %conditional.3 = ((f32[24,1,400,128]{3,2,1,0:T(8,128)}, f32[24,1,400,128]{3,2,1,0:T(8,128)})) conditional(s32[]{:T(128)} %convert_element_type.23, (s32[4,128]{1,0:T(4,128)}, f32[400,128]{1,0:T(8,128)S(1)}, f32[6,128]{1,0:T(8,128)}, bf16[4,1664,128]{2,1,0:T(8,128)(2,1)}, s16[2,416,128]{2,1,0:T(8,128)(2,1)S(1)}, ...), branch_computations={%region_4.5_spmd, %region_5.6_spmd} | conditional | bytes 4915412 | solution.py:859
  115.8 4.1 %update_tiles.3 = (f32[24,1,400,128]{3,2,1,0:T(8,128)}, f32[24,1,400,128]{3,2,1,0:T(8,128)}) custom-call(s32[4,128]{1,0:T(4,128)} %get-tuple-element.81.notes, f32[400,128]{1,0:T(8,128)S(1)} %get-tuple-element.82.occ_cols, f32[6,128]{1,0:T(8,128)} %get-tuple-element.83.vir_energy, ...), custom_call_target="tpu_custom_call", output_to_operand_aliasing={{0}: (16, {}), {1}: (17, {})} | custom-call | tf_op jit(solution)/shard_map/cond/branch_0_fun/update_tiles/pallas_call | solution.py:27
  (41 shorter events, 3.4 us)
Async XLA Ops:
  0.6 16.4 %copy-start = (bf16[4,400,6,128]{3,1,2,0:T(8,128)(2,1)S(1)}, bf16[4,400,6,128]{3,1,2,0:T(8,128)(2,1)}, u32[]{:S(2)}) copy-start(bf16[4,400,6,128]{3,1,2,0:T(8,128)(2,1)} %param.14) | copy-start | bytes 7372804
  0.6 15.8 %collective-permute-start.6 = (bf16[6,128,24,128]{3,2,1,0:T(8,128)(2,1)}, bf16[6,128,24,128]{3,2,1,0:T(8,128)(2,1)}, u32[]{:S(2)}, u32[]{:S(2)}) collective-permute-start(bf16[6,128,24,128]{3,2,1,0:T(8,128)(2,1)} %ints_own.7), channel_id=1, source_target_pairs={{0,1},{1,0},{2,3},{3,2},{4,5},{5,4},{6,7},{7,6},{8,9},{9,8},{10,11... | collective-permute-start | bytes 14155784 | tf_op jit(solution)/shard_map/ppermute | solution.py:654
  1.2 15.3 %collective-permute-start.5 = (bf16[24,400,128]{2,1,0:T(8,128)(2,1)}, bf16[24,400,128]{2,1,0:T(8,128)(2,1)}, u32[]{:S(2)}, u32[]{:S(2)}) collective-permute-start(bf16[24,400,128]{2,1,0:T(8,128)(2,1)} %bitcast.29), channel_id=1, source_target_pairs={{0,1},{1,0},{2,3},{3,2},{4,5},{5,4},{6,7},{7,6},{8,9},{9,8},{10,11... | collective-permute-start | bytes 7372808 | tf_op jit(solution)/shard_map/ppermute | solution.py:654
  6.6 48.1 %all-to-all-start = ((bf16[4,1664,128]{2,1,0:T(8,128)(2,1)}), bf16[4,1664,128]{2,1,0:T(8,128)(2,1)}, u32[]{:S(2)}, u32[]{:S(2)}) async-start(bf16[4,1664,128]{2,1,0:T(8,128)(2,1)} %get-tuple-element.156), calls=%async_computation | async-start | bytes 3407872 | tf_op jit(solution)/shard_map/all_to_all | solution.py:699
  12.7 1.8 %collective-permute-start.4 = (s32[16]{0:T(128)}, s32[16]{0:T(128)S(1)}, u32[]{:S(2)}, u32[]{:S(2)}) collective-permute-start(s32[16]{0:T(128)} %get-tuple-element.161), channel_id=1, source_target_pairs={{0,1},{1,0},{2,3},{3,2},{4,5},{5,4},{6,7},{7,6},{8,9},{9,8},{10,11... | collective-permute-start | bytes 200 | tf_op jit(solution)/shard_map/ppermute | solution.py:654
  12.7 3.8 %collective-permute-start.7 = (s32[24]{0:T(128)}, s32[24]{0:T(128)S(1)}, u32[]{:S(2)}, u32[]{:S(2)}) collective-permute-start(s32[24]{0:T(128)} %get-tuple-element.176.wanted), channel_id=1, source_target_pairs={{0,2},{1,3},{2,0},{3,1},{4,6},{5,7},{6,4},{7,5},{8,10},{9,11},{10,... | collective-permute-start | bytes 296 | tf_op jit(solution)/shard_map/ppermute | solution.py:654
  14.5 2.0 %copy-start.6 = (s32[16]{0:T(128)}, s32[16]{0:T(128)S(1)}, u32[]{:S(2)}) copy-start(s32[16]{0:T(128)S(1)} %collective-permute-done.4.mask_other) | copy-start | bytes 196
  16.5 0.6 copy-start.8
  25.9 24.2 %collective-permute-start.8 = (s16[8,416,128]{2,1,0:T(8,128)(2,1)}, s16[8,416,128]{2,1,0:T(8,128)(2,1)S(1)}, u32[]{:S(2)}, u32[]{:S(2)}) collective-permute-start(s16[8,416,128]{2,1,0:T(8,128)(2,1)} %ladder_sums.2), channel_id=1, source_target_pairs={{0,2},{1,3},{2,0},{3,1},{4,6},{5,7},{6,4},{7,5},{8,10},{9,11},{10,... | collective-permute-start | bytes 2555912 | tf_op jit(solution)/shard_map/ppermute | solution.py:654
  35.4 36.9 %collective-permute-start.12 = (s16[8,416,128]{2,1,0:T(8,128)(2,1)}, s16[8,416,128]{2,1,0:T(8,128)(2,1)}, u32[]{:S(2)}, u32[]{:S(2)}) collective-permute-start(s16[8,416,128]{2,1,0:T(8,128)(2,1)} %get-tuple-element.169), channel_id=1, source_target_pairs={{0,2},{1,3},{2,0},{3,1},{4,6},{5,7},{6,4},{7,5},{8,10},{9,11},{10,... | collective-permute-start | bytes 2555912 | tf_op jit(solution)/shard_map/ppermute | solution.py:654
  36.6 11.9 %copy-start.9 = (s32[24]{0:T(128)S(1)}, s32[24]{0:T(128)}, u32[]{:S(2)}) copy-start(s32[24]{0:T(128)} %copy-done.8) | copy-start | bytes 292
  36.6 11.9 %copy-start.10 = (s32[24]{0:T(128)S(1)}, s32[24]{0:T(128)}, u32[]{:S(2)}) copy-start(s32[24]{0:T(128)} %get-tuple-element.176.wanted) | copy-start | bytes 292
  36.6 39.8 %collective-permute-start.16 = (s16[4,416,128]{2,1,0:T(8,128)(2,1)}, s16[4,416,128]{2,1,0:T(8,128)(2,1)}, u32[]{:S(2)}, u32[]{:S(2)}) collective-permute-start(s16[4,416,128]{2,1,0:T(8,128)(2,1)} %get-tuple-element.175), channel_id=1, source_target_pairs={{0,2},{1,3},{2,0},{3,1},{4,6},{5,7},{6,4},{7,5},{8,10},{9,11},{10,... | collective-permute-start | bytes 1277960 | tf_op jit(solution)/shard_map/ppermute | solution.py:654
  50.0 0.9 copy-start.1
  56.8 23.7 %collective-permute-start.9 = (s16[2,416,128]{2,1,0:T(8,128)(2,1)}, s16[2,416,128]{2,1,0:T(8,128)(2,1)S(1)}, u32[]{:S(2)}, u32[]{:S(2)}) collective-permute-start(s16[2,416,128]{2,1,0:T(8,128)(2,1)} %get-tuple-element.164), channel_id=1, source_target_pairs={{0,12},{4,8},{8,4},{12,0},{1,13},{5,9},{9,5},{13,1},{2,14},{6,10},... | collective-permute-start | bytes 638984 | tf_op jit(solution)/shard_map/ppermute | solution.py:654
  59.6 24.2 %collective-permute-start.10 = (s16[2,416,128]{2,1,0:T(8,128)(2,1)}, s16[2,416,128]{2,1,0:T(8,128)(2,1)S(1)}, u32[]{:S(2)}, u32[]{:S(2)}) collective-permute-start(s16[2,416,128]{2,1,0:T(8,128)(2,1)} %get-tuple-element.165), channel_id=1, source_target_pairs={{0,8},{4,12},{8,0},{12,4},{1,9},{5,13},{9,1},{13,5},{2,10},{6,14},... | collective-permute-start | bytes 638984 | tf_op jit(solution)/shard_map/ppermute | solution.py:654
  61.1 22.8 %collective-permute-start.11 = (s16[2,416,128]{2,1,0:T(8,128)(2,1)}, s16[2,416,128]{2,1,0:T(8,128)(2,1)S(1)}, u32[]{:S(2)}, u32[]{:S(2)}) collective-permute-start(s16[2,416,128]{2,1,0:T(8,128)(2,1)} %get-tuple-element.166), channel_id=1, source_target_pairs={{0,4},{4,0},{8,12},{12,8},{1,5},{5,1},{9,13},{13,9},{2,6},{6,2},{1... | collective-permute-start | bytes 638984 | tf_op jit(solution)/shard_map/ppermute | solution.py:654
  76.4 4.1 %copy-start.7 = (f32[4,1,1,128]{3,2,1,0:T(1,128)S(1)}, f32[4,1,1,128]{3,2,1,0:T(1,128)}, u32[]{:S(2)}) copy-start(f32[4,1,1,128]{3,2,1,0:T(1,128)} %slice.32) | copy-start | bytes 6148
  79.2 10.5 %collective-permute-start.17 = (s16[2,416,128]{2,1,0:T(8,128)(2,1)}, s16[2,416,128]{2,1,0:T(8,128)(2,1)}, u32[]{:S(2)}, u32[]{:S(2)}) collective-permute-start(s16[2,416,128]{2,1,0:T(8,128)(2,1)} %get-tuple-element.181), channel_id=1, source_target_pairs={{0,12},{4,8},{8,4},{12,0},{1,13},{5,9},{9,5},{13,1},{2,14},{6,10},... | collective-permute-start | bytes 638984 | tf_op jit(solution)/shard_map/ppermute | solution.py:654
  79.3 32.5 %collective-permute-start.18 = (s16[2,416,128]{2,1,0:T(8,128)(2,1)}, s16[2,416,128]{2,1,0:T(8,128)(2,1)}, u32[]{:S(2)}, u32[]{:S(2)}) collective-permute-start(s16[2,416,128]{2,1,0:T(8,128)(2,1)} %get-tuple-element.182), channel_id=1, source_target_pairs={{0,8},{4,12},{8,0},{12,4},{1,9},{5,13},{9,1},{13,5},{2,10},{6,14},... | collective-permute-start | bytes 638984 | tf_op jit(solution)/shard_map/ppermute | solution.py:654
  80.5 18.4 %copy-start.5 = (s32[4,128]{1,0:T(4,128)}, s32[4,128]{1,0:T(4,128)S(1)}, u32[]{:S(2)}) copy-start(s32[4,128]{1,0:T(4,128)S(1)} %convert_bitcast_fusion.notes) | copy-start | bytes 6148
  80.5 31.3 %collective-permute-start.19 = (s16[2,416,128]{2,1,0:T(8,128)(2,1)}, s16[2,416,128]{2,1,0:T(8,128)(2,1)}, u32[]{:S(2)}, u32[]{:S(2)}) collective-permute-start(s16[2,416,128]{2,1,0:T(8,128)(2,1)} %get-tuple-element.183), channel_id=1, source_target_pairs={{0,4},{4,0},{8,12},{12,8},{1,5},{5,1},{9,13},{13,9},{2,6},{6,2},{1... | collective-permute-start | bytes 638984 | tf_op jit(solution)/shard_map/ppermute | solution.py:654
  83.8 28.0 %collective-permute-start.13 = (s16[2,416,128]{2,1,0:T(8,128)(2,1)}, s16[2,416,128]{2,1,0:T(8,128)(2,1)}, u32[]{:S(2)}, u32[]{:S(2)}) collective-permute-start(s16[2,416,128]{2,1,0:T(8,128)(2,1)} %get-tuple-element.171), channel_id=1, source_target_pairs={{0,12},{4,8},{8,4},{12,0},{1,13},{5,9},{9,5},{13,1},{2,14},{6,10},... | collective-permute-start | bytes 638984 | tf_op jit(solution)/shard_map/ppermute | solution.py:654
  83.9 31.9 %collective-permute-start.14 = (s16[2,416,128]{2,1,0:T(8,128)(2,1)}, s16[2,416,128]{2,1,0:T(8,128)(2,1)}, u32[]{:S(2)}, u32[]{:S(2)}) collective-permute-start(s16[2,416,128]{2,1,0:T(8,128)(2,1)} %get-tuple-element.172), channel_id=1, source_target_pairs={{0,8},{4,12},{8,0},{12,4},{1,9},{5,13},{9,1},{13,5},{2,10},{6,14},... | collective-permute-start | bytes 638984 | tf_op jit(solution)/shard_map/ppermute | solution.py:654
  89.7 26.1 %collective-permute-start.15 = (s16[2,416,128]{2,1,0:T(8,128)(2,1)}, s16[2,416,128]{2,1,0:T(8,128)(2,1)}, u32[]{:S(2)}, u32[]{:S(2)}) collective-permute-start(s16[2,416,128]{2,1,0:T(8,128)(2,1)} %get-tuple-element.173), channel_id=1, source_target_pairs={{0,4},{4,0},{8,12},{12,8},{1,5},{5,1},{9,13},{13,9},{2,6},{6,2},{1... | collective-permute-start | bytes 638984 | tf_op jit(solution)/shard_map/ppermute | solution.py:654
